TPU v7x, 256 devices: a whole 4x4x8 slice. The times are simulated.
256 devices in a mesh: qa: 32 (over y, z_lo, core), qb: 8 (over z_hi, x).
Axes of the slice: x: 4, y: 4, z: 8 (z_hi: 2, z_lo: 4; z = z_hi * 4 + z_lo), core: 2. Of those that a mesh axis runs over, the one named last changes fastest.
Arguments:
- amplitudes: float32 [2, 16777216], P(None, ('qa', 'qb')), may hold values from -6 to 6
- gate_mats: float32 [6, 2, 128, 128], replicated, may hold values from -0.375 to 0.375
- gate_order: int32 [6, 7], replicated, may hold values from 0 to 6, each once within a row
- phase_pairs: int32 [3, 4, 2], replicated, may hold values from 0 to 23
- phase_angles: float32 [3, 4], replicated, may hold values from -3.140625 to 3.140625
Outputs:
- evolved: float32 [2, 16777216], P(None, ('qa', 'qb'))
Inputs may be any that keep to these rules, and one draw needn't show every extreme that they name: `gate_order`: each row is an order of the 7 qubits of one merged gate. `phase_pairs`: qubit numbers below 24; the two of a coupling may coincide.
All inputs are finite; a program needn't handle non-finite values.
Results may differ from a plain program's by a relative error of at most 0.0001.
Values sent between devices are 32-bit elements; how exact they have to be, the bound alone decides.
No kernel may reach another device: no remote copies, remote signals or barrier semaphores. Data moves between devices by JAX's collectives and lax.ppermute only.
A program may use at most 64 MiB of HBM per device.

v0:
```python
import itertools

import jax
import jax.numpy as jnp
from jax import lax
from jax.experimental import pallas as pl
from jax.experimental.pallas import tpu as pltpu
from jax.sharding import PartitionSpec as P

AXES = ("qa", "qb")
SIZES = {"y": 4, "zl": 4, "c": 2, "zh": 2, "x": 4}
F32 = jnp.float32
BF16 = jnp.bfloat16
LANES = 128


def device_groups(varying):
    fixed = [name for name in SIZES if name not in varying]
    groups = []
    for held in itertools.product(*[range(SIZES[name]) for name in fixed]):
        group = []
        for moved in itertools.product(*[range(SIZES[name]) for name in varying]):
            at = dict(zip(fixed, held)) | dict(zip(varying, moved))
            group.append((at["y"] * 8 + at["zl"] * 2 + at["c"]) * 8 + at["zh"] * 4 + at["x"])
        groups.append(group)
    return groups


def exchange(values, varying):
    groups = device_groups(varying)
    parts = values.reshape(len(groups[0]), -1, LANES)
    if len(groups) == 1:
        moved = lax.all_to_all(parts, AXES, 0, 0, tiled=True)
    else:
        moved = lax.all_to_all(parts, AXES, 0, 0, axis_index_groups=groups, tiled=True)
    return moved.reshape(values.shape)


def iota(axis, shape=(128, 128)):
    return lax.broadcasted_iota(jnp.int32, shape, axis)


def take_bits(index, places):
    total = None
    for source, place in enumerate(places):
        bit = jnp.left_shift(jnp.bitwise_and(jnp.right_shift(index, source), 1), place)
        total = bit if total is None else total + bit
    return total


def onehot(order_ref, gate, places, axis):
    index = take_bits(iota(axis), places)
    mapped = None
    for target in range(7):
        bit = jnp.bitwise_and(jnp.right_shift(index, order_ref[gate, target]), 1)
        bit = jnp.left_shift(bit, target)
        mapped = bit if mapped is None else mapped + bit
    return (mapped == iota(1 - axis)).astype(F32).astype(BF16)


def mul(left, right):
    return jnp.dot(left, right, preferred_element_type=F32)


def mul_t(left, right):
    return lax.dot_general(left, right, (((1,), (1,)), ((), ())), preferred_element_type=F32)


def halves(values):
    high = values.astype(BF16)
    return high, (values - high.astype(F32)).astype(BF16)


NATURAL = tuple(range(7))


def gate_block(mats_ref, order_ref, gate, row_places=NATURAL, column_places=NATURAL):
    rows = onehot(order_ref, gate, row_places, 0)
    columns = onehot(order_ref, gate, column_places, 1)
    blocks = []
    real, imag = [halves(mats_ref[gate, part]) for part in range(2)]
    for real_half, imag_half in zip(real, imag):
        both = jnp.concatenate([real_half, imag_half], axis=0)
        both = mul(both, columns).astype(BF16)
        vr = mul(rows, both[:128]).astype(BF16)
        vi = mul(rows, both[128:]).astype(BF16)
        blocks.append((vr, vi))
    return blocks


def full_block(blocks):
    out = []
    for vr, vi in blocks:
        out.append(
            jnp.concatenate(
                [jnp.concatenate([vr, -vi], axis=1), jnp.concatenate([vi, vr], axis=1)], axis=0
            )
        )
    return out


def product(multiply, block, values, values_left=False):
    high, low = halves(values)
    block_high, block_low = block
    if values_left:
        return multiply(high, block_high) + (multiply(low, block_high) + multiply(high, block_low))
    return multiply(block_high, high) + (multiply(block_high, low) + multiply(block_low, high))


def sign_of(index, pairs_ref, layer, term):
    first = jnp.right_shift(index, pairs_ref[layer, term, 0])
    second = jnp.right_shift(index, pairs_ref[layer, term, 1])
    bit = jnp.bitwise_and(jnp.bitwise_xor(first, second), 1)
    return (1 - 2 * bit).astype(F32)


class Phase:
    def __init__(self, pairs_ref, angles_ref, layer, index):
        self.pairs_ref = pairs_ref
        self.layer = layer
        angles = angles_ref[...]
        cosine = jnp.cos(angles)
        sine = jnp.sin(angles)
        self.cosine = [cosine[layer : layer + 1, term : term + 1] for term in range(4)]
        self.sine = [
            sine[layer : layer + 1, term : term + 1] * sign_of(index, pairs_ref, layer, term)
            for term in range(4)
        ]

    def __call__(self, real, imag, rest):
        factors = []
        for term in range(4):
            sign = sign_of(rest, self.pairs_ref, self.layer, term)
            factors.append((self.cosine[term], self.sine[term] * sign))

        def pair(first, second):
            return (
                first[0] * second[0] - first[1] * second[1],
                first[0] * second[1] + first[1] * second[0],
            )

        cosine, sine = pair(pair(factors[0], factors[1]), pair(factors[2], factors[3]))
        return real * cosine - imag * sine, real * sine + imag * cosine


def swap_bit(tiles, tile_bit, lane_bit):
    width = 1 << lane_bit
    lane = iota(1, tiles[0].shape)
    low = jnp.bitwise_and(lane, width) == 0
    out = list(tiles)
    for number in range(len(tiles)):
        other = number | (1 << tile_bit)
        if other == number:
            continue
        first, second = tiles[number], tiles[other]
        out[number] = jnp.where(low, first, pltpu.roll(second, width, 1))
        out[other] = jnp.where(low, pltpu.roll(first, LANES - width, 1), second)
    return out


def place():
    qa = lax.axis_index("qa")
    qb = lax.axis_index("qb")
    return qa // 2, qa % 2, qb // 4, qb % 4


def kernel_a(amps_ref, mats_ref, order_ref, pairs_ref, angles_ref, out_ref):
    block = full_block(gate_block(mats_ref, order_ref, 1))
    yz, core, zh, x = place()
    device = yz * (1 << 20) + core * (1 << 19) + zh * (1 << 18) + x * (1 << 16)
    phase = Phase(pairs_ref, angles_ref, 0, iota(0) * 512 + iota(1))
    for mid in range(4):
        real = amps_ref[pl.ds(2 * mid, 128, stride=8), :]
        imag = amps_ref[pl.ds(2 * mid + 1, 128, stride=8), :]
        real, imag = phase(real, imag, device + mid * 128)
        values = jnp.concatenate([real, imag], axis=1)
        result = product(mul_t, block, values)
        for part in range(2):
            tiles = result[part * 128 : (part + 1) * 128].reshape(16, 8, LANES)
            out_ref[mid * 16 : (mid + 1) * 16, part * 8 : (part + 1) * 8, :] = tiles


def kernel_b(amps_ref, mats_ref, order_ref, pairs_ref, angles_ref, out_ref):
    yz, core, zh, x = place()
    device = yz * (1 << 4) + core * (1 << 3) + zh * (1 << 8) + x * (1 << 16)
    block_0 = full_block(gate_block(mats_ref, order_ref, 0))
    columns = []
    for u in range(4):
        parts = []
        for part in range(2):
            start = (u // 2) * 512 + part * 8 + (u % 2) * 4
            tiles = [amps_ref[pl.ds(start + t, 32, stride=16), :] for t in range(4)]
            tiles = swap_bit(swap_bit(tiles, 1, 6), 0, 5)
            parts += tiles
        columns.append(jnp.concatenate(parts, axis=0))
    result = product(mul, block_0, jnp.concatenate(columns, axis=1))
    row, lane = iota(0), iota(1)
    index = (row // 32) * (1 << 14) + (row % 32) * (1 << 19) + (lane // 32) + (lane % 32) * 512
    phase = Phase(pairs_ref, angles_ref, 1, index)
    block_3 = gate_block(mats_ref, order_ref, 3)
    block_3 = [
        jnp.concatenate(
            [
                jnp.concatenate([vr, -vi], axis=1).reshape(32, 4, 256),
                jnp.concatenate([vi, vr], axis=1).reshape(32, 4, 256),
            ],
            axis=1,
        ).reshape(256, 256)
        for vr, vi in [(vr.astype(F32), vi.astype(F32)) for vr, vi in block_3]
    ]
    block_3 = [half.astype(BF16) for half in block_3]
    rows = []
    for u in range(4):
        real = result[:128, u * 128 : (u + 1) * 128]
        imag = result[128:, u * 128 : (u + 1) * 128]
        parts = []
        for value in phase(real, imag, device + (u // 2) * (1 << 18) + (u % 2) * 4):
            tiles = [value[ah * 32 : (ah + 1) * 32] for ah in range(4)]
            tiles = swap_bit(swap_bit(tiles, 1, 6), 0, 5)
            parts.append(jnp.concatenate(tiles, axis=0))
        rows.append(jnp.concatenate(parts, axis=1))
    result = product(mul_t, block_3, jnp.concatenate(rows, axis=0))
    for u in range(4):
        values = result[:, u * 128 : (u + 1) * 128]
        tiles = [values[ah * 64 : (ah + 1) * 64] for ah in range(4)]
        tiles = swap_bit(swap_bit(tiles, 1, 6), 0, 5)
        for t in range(4):
            out_ref[:, u * 4 + t, :, :] = tiles[t].reshape(8, 8, LANES)


def kernel_c(amps_ref, mats_ref, order_ref, pairs_ref, angles_ref, out_ref):
    yz, core, zh, x = place()
    device = yz * (1 << 4) + core * (1 << 11) + zh * (1 << 8) + x * (1 << 12)
    block_2 = full_block(gate_block(mats_ref, order_ref, 2, NATURAL, (0, 1, 2, 6, 3, 4, 5)))
    columns = []
    for xl in range(4):
        columns.append(
            jnp.concatenate(
                [amps_ref[pl.ds(part * 4 + xl, 128, stride=8), :] for part in range(2)], axis=0
            )
        )
    result = product(mul, block_2, jnp.concatenate(columns, axis=1))
    row, lane = iota(0), iota(1)
    index = (row // 16) * (1 << 16) + (row % 16) + (lane // 32) * (1 << 14) + (lane % 32) * (1 << 19)
    phase = Phase(pairs_ref, angles_ref, 2, index)
    block_4 = full_block(gate_block(mats_ref, order_ref, 4))
    rotated = [
        phase(
            result[:128, xl * 128 : (xl + 1) * 128],
            result[128:, xl * 128 : (xl + 1) * 128],
            device + xl * 512,
        )
        for xl in range(4)
    ]
    rows = []
    for gb in range(8):
        for xl in range(4):
            real, imag = rotated[xl]
            rows.append(
                jnp.concatenate(
                    [real[gb * 16 : (gb + 1) * 16], imag[gb * 16 : (gb + 1) * 16]], axis=1
                )
            )
    result = product(mul_t, block_4, jnp.concatenate(rows, axis=0))
    for pair in range(4):
        values = result[:, pair * 128 : (pair + 1) * 128]
        tiles = swap_bit([values[:128], values[128:]], 0, 6)
        for last in range(2):
            gb = pair * 2 + last
            for ah in range(4):
                out_ref[pl.ds(gb * 4 + ah, 32, stride=32), :] = tiles[last][ah * 32 : (ah + 1) * 32]


def kernel_d(amps_ref, mats_ref, order_ref, out_ref):
    block = full_block(gate_block(mats_ref, order_ref, 5))
    rows = []
    for b7 in range(2):
        start = b7 * 512
        tiles = [amps_ref[start + xb * 64 : start + (xb + 1) * 64, :] for xb in range(8)]
        tiles = swap_bit(swap_bit(swap_bit(tiles, 2, 6), 1, 5), 0, 4)
        for xl in range(4):
            rows.append(jnp.concatenate([tiles[xl], tiles[4 + xl]], axis=1))
    result = product(mul_t, block, jnp.concatenate(rows, axis=0), values_left=True)
    for b7 in range(2):
        for xl in range(4):
            start = (b7 * 4 + xl) * 64
            for b11, b8, b13, b12 in itertools.product(range(2), repeat=4):
                at = start + b11 * 32 + b8 * 16 + b13 * 8 + b12 * 4
                to = b13 * 64 + b12 * 32 + b11 * 16 + xl * 4 + b8 * 2 + b7
                for part in range(2):
                    out_ref[pl.ds(2 * to + part, 4, stride=256), :] = result[
                        at : at + 4, part * 128 : (part + 1) * 128
                    ]


def call(kernel, name, shape, operands, scalars):
    return pl.pallas_call(
        kernel,
        out_shape=jax.ShapeDtypeStruct(shape, F32),
        in_specs=[pl.BlockSpec(memory_space=pltpu.VMEM)] * 2
        + [pl.BlockSpec(memory_space=pltpu.SMEM)] * (scalars if scalars < 2 else 2)
        + ([pl.BlockSpec(memory_space=pltpu.VMEM)] if scalars > 2 else []),
        out_specs=pl.BlockSpec(memory_space=pltpu.VMEM),
        compiler_params=pltpu.CompilerParams(vmem_limit_bytes=24 * 1024 * 1024),
        cost_estimate=pl.CostEstimate(flops=400_000_000, bytes_accessed=2_000_000, transcendentals=0),
        name=name,
    )(*operands)


def body(amplitudes, gate_mats, gate_order, phase_pairs, phase_angles):
    shared = (gate_mats, gate_order, phase_pairs, phase_angles)
    state = amplitudes.reshape(2, 512, LANES).transpose(1, 0, 2).reshape(1024, LANES)
    state = call(kernel_a, "first_gate", (64, 16, LANES), (state, *shared), 3)
    state = exchange(state, ["zh", "y", "zl", "c"]).reshape(1024, LANES)
    state = call(kernel_b, "second_gates", (8, 16, 8, LANES), (state, *shared), 3)
    state = exchange(state.reshape(1024, LANES), ["x", "c"])
    state = call(kernel_c, "third_gates", (1024, LANES), (state, *shared), 3)
    state = exchange(state, ["y", "zl", "c", "zh", "x"])
    state = call(kernel_d, "last_gate", (1024, LANES), (state, gate_mats, gate_order), 1)
    return state.reshape(512, 2, LANES).transpose(1, 0, 2).reshape(2, 65536)


def solution(mesh):
    return jax.shard_map(
        body,
        mesh=mesh,
        in_specs=(P(None, AXES), P(), P(), P(), P()),
        out_specs=P(None, AXES),
        check_vma=False,
    )
```

profile of v0, /device:TPU:1, one launch (start us, length us, event | category | flops | bytes accessed | tf_op | source)
XLA Modules:
  0.0 84.0 jit_solution(9932584979003007430)
XLA Ops:
  0.0 0.0 copy-start.3
  0.0 0.0 copy-start.4
  0.0 0.8 copy.7.pairs_ref
  0.8 0.0 copy-done.3
  0.8 0.0 copy-done.4
  0.8 0.0 copy-start
  0.8 1.1 %copy-done = f32[6,2,128,128]{3,2,1,0:T(8,128)S(1)} copy-done((f32[6,2,128,128]{3,2,1,0:T(8,128)S(1)}, f32[6,2,128,128]{3,2,1,0:T(8,128)}, u32[]{:S(2)}) %copy-start) | copy-done | bytes 786456
  2.0 0.0 copy-start.2
  2.0 1.0 %copy-done.2 = f32[2,65536]{1,0:T(2,128)S(1)} copy-done((f32[2,65536]{1,0:T(2,128)S(1)}, f32[2,65536]{1,0:T(2,128)}, u32[]{:S(2)}) %copy-start.2) | copy-done | bytes 524312
  3.0 1.7 %first_gate.1 = f32[64,16,128]{2,1,0:T(8,128)S(1)} custom-call(f32[1024,128]{1,0:T(8,128)S(1)} %bitcast.20, f32[6,2,128,128]{3,2,1,0:T(8,128)S(1)} %copy-done, s32[6,7]{1,0:T(8,128)S(1)} %copy-done.3, s32[3,4,2]{2,1,0:T(4,128)S(1)} %copy.7.pairs_ref, f32[3,4]{1,0:T(4,128)S(1)} %copy-done.4), custom_call_target="tpu_custom_call" | custom-call | flops 400000000 | bytes 2000000 | tf_op jit(solution)/shard_map/first_gate/pallas_call | solution.py:297
  4.7 0.0 copy-start.1
  4.7 31.9 %all_to_all.15 = f32[64,16,128]{2,1,0:T(8,128)S(1)} all-to-all(f32[64,16,128]{2,1,0:T(8,128)S(1)} %first_gate.1), channel_id=1, replica_groups={{0,8,16,24,32,40,48,56,64,72,80,88,96,104,112,120,128,136,144,152,160,1..., dimensions={0} | all-to-all | bytes 1048576 | tf_op jit(solution)/shard_map/all_to_all | solution.py:35
  36.6 0.0 copy-done.1
  36.6 2.7 %second_gates.1 = f32[8,16,8,128]{3,2,1,0:T(8,128)S(1)} custom-call(f32[1024,128]{1,0:T(8,128)S(1)} %bitcast.17, f32[6,2,128,128]{3,2,1,0:T(8,128)S(1)} %copy-done.1, s32[6,7]{1,0:T(8,128)S(1)} %copy-done.3, s32[3,4,2]{2,1,0:T(4,128)S(1)} %copy.7.pairs_ref, f32[3,4]{1,0:T(4,128)S(1)} %copy-done.4), custom_call_target="tpu_custom_call" | custom-call | flops 400000000 | bytes 2000000 | tf_op jit(solution)/shard_map/second_gates/pallas_call | solution.py:297
  39.3 13.6 %all_to_all.16 = f32[8,128,128]{2,1,0:T(8,128)S(1)} all-to-all(f32[8,128,128]{2,1,0:T(8,128)S(1)} %bitcast.18), channel_id=1, replica_groups={{0,8,1,9,2,10,3,11},{4,12,5,13,6,14,7,15},{16,24,17,25,18,26,19,27},{20..., dimensions={0} | all-to-all | bytes 1048576 | tf_op jit(solution)/shard_map/all_to_all | solution.py:35
  52.9 2.7 %third_gates.1 = f32[1024,128]{1,0:T(8,128)S(1)} custom-call(f32[1024,128]{1,0:T(8,128)S(1)} %bitcast.15, f32[6,2,128,128]{3,2,1,0:T(8,128)S(1)} %copy-done.1, s32[6,7]{1,0:T(8,128)S(1)} %copy-done.3, s32[3,4,2]{2,1,0:T(4,128)S(1)} %copy.7.pairs_ref, f32[3,4]{1,0:T(4,128)S(1)} %copy-done.4), custom_call_target="tpu_custom_call" | custom-call | flops 400000000 | bytes 2000000 | tf_op jit(solution)/shard_map/third_gates/pallas_call | solution.py:297
  55.6 26.0 %all_to_all.17 = f32[256,4,128]{2,1,0:T(4,128)S(1)} all-to-all(f32[256,4,128]{2,1,0:T(4,128)S(1)} %bitcast.16), channel_id=1, replica_groups=mesh['qa'=32,'qb'=8] {'qa','qb'}, dimensions={0} | all-to-all | bytes 1048576 | tf_op jit(solution)/shard_map/all_to_all | solution.py:33
  81.6 2.4 %last_gate.1 = f32[1024,128]{1,0:T(8,128)} custom-call(f32[1024,128]{1,0:T(8,128)S(1)} %bitcast.19, f32[6,2,128,128]{3,2,1,0:T(8,128)S(1)} %copy-done.1, s32[6,7]{1,0:T(8,128)S(1)} %copy-done.3), custom_call_target="tpu_custom_call" | custom-call | flops 400000000 | bytes 2000000 | tf_op jit(solution)/shard_map/last_gate/pallas_call | solution.py:297
Async XLA Ops:
  0.0 0.8 copy-start.3
  0.0 0.8 copy-start.4
  0.8 1.1 %copy-start = (f32[6,2,128,128]{3,2,1,0:T(8,128)S(1)}, f32[6,2,128,128]{3,2,1,0:T(8,128)}, u32[]{:S(2)}) copy-start(f32[6,2,128,128]{3,2,1,0:T(8,128)} %mats_ref.7) | copy-start | bytes 2359300
  2.0 1.0 %copy-start.2 = (f32[2,65536]{1,0:T(2,128)S(1)}, f32[2,65536]{1,0:T(2,128)}, u32[]{:S(2)}) copy-start(f32[2,65536]{1,0:T(2,128)} %param.5) | copy-start | bytes 1572868
  4.7 31.9 %copy-start.1 = (f32[6,2,128,128]{3,2,1,0:T(8,128)S(1)}, f32[6,2,128,128]{3,2,1,0:T(8,128)}, u32[]{:S(2)}) copy-start(f32[6,2,128,128]{3,2,1,0:T(8,128)} %mats_ref.7) | copy-start | bytes 2359300
where the time goes:
time: 84.3 us; the launch traced here: 84 us
  blocking collectives  71.4 us (85%)
  Pallas kernels  9.56 us (11%)
  local copies, waits for them, and re-layouts  2.99 us (4%)
    all_to_all x2, blocking collectives, exchange(): lax.all_to_all(parts, AXES, 0, 0, axis_index_groups=groups, tiled=True)  45.5 us
    all_to_all x1, blocking collectives, exchange(): moved = lax.all_to_all(parts, AXES, 0, 0, tiled=True)  26 us
    pallas_call x4, Pallas kernels, call(): pl.pallas_call(kernel, out_shape=jax.ShapeDtypeStruct(shape, F32), in_spe...  9.56 us
    unnamed x11, local copies, waits for them, and re-layouts  2.99 us

commit v1 on v0

v1 whole, which is shorter than its diff:
```python
import itertools

import jax
import jax.numpy as jnp
from jax import lax
from jax.experimental import pallas as pl
from jax.experimental.pallas import tpu as pltpu
from jax.sharding import PartitionSpec as P

AXES = ("qa", "qb")
SIZES = {"y": 4, "zl": 4, "c": 2, "zh": 2, "x": 4}
F32 = jnp.float32
BF16 = jnp.bfloat16
LANES = 128


def device_groups(varying):
    fixed = [name for name in SIZES if name not in varying]
    groups = []
    for held in itertools.product(*[range(SIZES[name]) for name in fixed]):
        group = []
        for moved in itertools.product(*[range(SIZES[name]) for name in varying]):
            at = dict(zip(fixed, held)) | dict(zip(varying, moved))
            group.append((at["y"] * 8 + at["zl"] * 2 + at["c"]) * 8 + at["zh"] * 4 + at["x"])
        groups.append(group)
    return groups


def exchange(values, varying):
    groups = device_groups(varying)
    parts = values.reshape(len(groups[0]), -1, LANES)
    if len(groups) == 1:
        moved = lax.all_to_all(parts, AXES, 0, 0, tiled=True)
    else:
        moved = lax.all_to_all(parts, AXES, 0, 0, axis_index_groups=groups, tiled=True)
    return moved.reshape(values.shape)


def iota(axis, shape=(128, 128)):
    return lax.broadcasted_iota(jnp.int32, shape, axis)


def take_bits(index, places):
    total = None
    for source, place in enumerate(places):
        bit = jnp.left_shift(jnp.bitwise_and(jnp.right_shift(index, source), 1), place)
        total = bit if total is None else total + bit
    return total


def onehot(order_ref, gate, index):
    mapped = None
    order = order_ref[...]
    for target in range(7):
        shift = order[gate : gate + 1, target : target + 1]
        bit = jnp.bitwise_and(jnp.right_shift(index, shift), 1)
        bit = jnp.left_shift(bit, target)
        mapped = bit if mapped is None else mapped + bit
    return (mapped == iota(1)).astype(F32).astype(BF16)


def mul(left, right):
    return jnp.dot(left, right, preferred_element_type=F32)


def mul_t(left, right):
    return lax.dot_general(left, right, (((1,), (1,)), ((), ())), preferred_element_type=F32)


def halves(values):
    high = values.astype(BF16)
    return high, (values - high.astype(F32)).astype(BF16)


def gate_block(mats, order_ref, gate, rows=None, columns=None):
    rows = onehot(order_ref, gate, iota(0) if rows is None else rows)
    columns = rows if columns is None else onehot(order_ref, gate, columns)
    parts = [half for part in range(2) for half in halves(mats[part])]
    turned = mul_t(columns, jnp.concatenate(parts, axis=0)).astype(BF16)
    parts = [mul_t(rows, turned[:, at * 128 : (at + 1) * 128]).astype(BF16) for at in range(4)]
    return [(parts[0], parts[2]), (parts[1], parts[3])]


def full_block(blocks):
    out = []
    for vr, vi in blocks:
        out.append(
            jnp.concatenate(
                [jnp.concatenate([vr, -vi], axis=1), jnp.concatenate([vi, vr], axis=1)], axis=0
            )
        )
    return out


def product(multiply, block, values, values_left=False):
    high, low = halves(values)
    block_high, block_low = block
    if values_left:
        return multiply(high, block_high) + (multiply(low, block_high) + multiply(high, block_low))
    return multiply(block_high, high) + (multiply(block_high, low) + multiply(block_low, high))


def sign_of(index, pairs, layer, term):
    first = jnp.right_shift(index, pairs[layer, 0:1, term : term + 1])
    second = jnp.right_shift(index, pairs[layer, 1:2, term : term + 1])
    bit = jnp.bitwise_and(jnp.bitwise_xor(first, second), 1)
    return (1 - 2 * bit).astype(F32)


class Phase:
    def __init__(self, pairs_ref, angles_ref, layer, index):
        self.pairs = pairs_ref[...]
        self.layer = layer
        angles = angles_ref[...]
        cosine = jnp.cos(angles)
        sine = jnp.sin(angles)
        self.cosine = [cosine[layer : layer + 1, term : term + 1] for term in range(4)]
        self.sine = [
            sine[layer : layer + 1, term : term + 1] * sign_of(index, self.pairs, layer, term)
            for term in range(4)
        ]

    def factor(self, rest):
        rest = jnp.full((1, 1), rest, jnp.int32)
        factors = []
        for term in range(4):
            sign = sign_of(rest, self.pairs, self.layer, term)
            factors.append((self.cosine[term], self.sine[term] * sign))

        def pair(first, second):
            return (
                first[0] * second[0] - first[1] * second[1],
                first[0] * second[1] + first[1] * second[0],
            )

        return pair(pair(factors[0], factors[1]), pair(factors[2], factors[3]))


def rotate(factor, real, imag):
    cosine, sine = factor
    return real * cosine - imag * sine, real * sine + imag * cosine


def swap_bit(tiles, tile_bit, lane_bit):
    width = 1 << lane_bit
    lane = iota(1, tiles[0].shape)
    low = jnp.bitwise_and(lane, width) == 0
    out = list(tiles)
    for number in range(len(tiles)):
        other = number | (1 << tile_bit)
        if other == number:
            continue
        first, second = tiles[number], tiles[other]
        out[number] = jnp.where(low, first, pltpu.roll(second, width, 1))
        out[other] = jnp.where(low, pltpu.roll(first, LANES - width, 1), second)
    return out


def place():
    qa = lax.axis_index("qa")
    qb = lax.axis_index("qb")
    return qa // 2, qa % 2, qb // 4, qb % 4


def kernel_a(
    amps_hbm, mats_hbm, order_hbm, pairs_hbm, angles_hbm, out_hbm,
    amps, mats, order, pairs, angles, out, sems, out_sems,
):
    sources = (mats_hbm.at[1], order_hbm, pairs_hbm, angles_hbm, amps_hbm)
    targets = (mats, order, pairs, angles, amps)
    copies = [
        pltpu.make_async_copy(source, target, sems.at[number])
        for number, (source, target) in enumerate(zip(sources, targets))
    ]
    for copy in copies:
        copy.start()
    for copy in copies[:4]:
        copy.wait()
    block = full_block(gate_block(mats, order, 1))
    yz, core, zh, x = place()
    device = yz * (1 << 20) + core * (1 << 19) + zh * (1 << 18) + x * (1 << 16)
    phase = Phase(pairs, angles, 0, iota(0) * 512 + iota(1))
    copies[4].wait()
    written = []
    for mid in range(4):
        real = amps[pl.ds(2 * mid, 128, stride=8), :]
        imag = amps[pl.ds(2 * mid + 1, 128, stride=8), :]
        real, imag = rotate(phase.factor(device + mid * 128), real, imag)
        values = jnp.concatenate([real, imag], axis=1)
        result = product(mul_t, block, values)
        for part in range(2):
            tiles = result[part * 128 : (part + 1) * 128].reshape(16, 8, LANES)
            out[mid * 16 : (mid + 1) * 16, part * 8 : (part + 1) * 8, :] = tiles
        piece = pl.ds(mid * 16, 16)
        written.append(pltpu.make_async_copy(out.at[piece], out_hbm.at[piece], out_sems.at[mid]))
        written[-1].start()
    for copy in written:
        copy.wait()


def kernel_tables(mats_ref, order_ref, pairs_ref, angles_ref, gates_ref, factors_ref):
    yz, core, zh, x = place()
    row, lane = iota(0), iota(1)
    index = (row // 32) * (1 << 14) + (row % 32) * (1 << 19) + (lane // 32) + (lane % 32) * 512
    phase = Phase(pairs_ref, angles_ref, 1, index)
    device = yz * (1 << 4) + core * (1 << 3) + zh * (1 << 8) + x * (1 << 16)
    for u in range(4):
        factor = phase.factor(device + (u // 2) * (1 << 18) + (u % 2) * 4)
        for part in range(2):
            factors_ref[0, part, u] = factor[part]
    index = (row // 16) * (1 << 16) + (row % 16) + (lane // 32) * (1 << 14) + (lane % 32) * (1 << 19)
    phase = Phase(pairs_ref, angles_ref, 2, index)
    device = yz * (1 << 4) + core * (1 << 11) + zh * (1 << 8) + x * (1 << 12)
    for xl in range(4):
        factor = phase.factor(device + xl * 512)
        for part in range(2):
            factors_ref[1, part, xl] = factor[part]
    natural = iota(0)
    arrived = take_bits(natural, (0, 1, 2, 6, 3, 4, 5))
    for slot, gate in enumerate((0, 3, 2, 4, 5)):
        rows = natural
        columns = arrived if gate == 2 else natural
        blocks = gate_block(
            mats_ref.at[gate], order_ref, gate, rows, None if rows is columns else columns
        )
        if gate == 3:
            for half, (vr, vi) in enumerate(blocks):
                vr, vi = vr.astype(F32), vi.astype(F32)
                top = jnp.concatenate([vr, -vi], axis=1).reshape(32, 4, 256)
                bottom = jnp.concatenate([vi, vr], axis=1).reshape(32, 4, 256)
                mixed = jnp.concatenate([top, bottom], axis=1).reshape(256, 256)
                gates_ref[slot, half] = mixed.astype(BF16)
        else:
            for half, block in enumerate(full_block(blocks)):
                gates_ref[slot, half] = block


def kernel_b(amps_ref, gates_ref, factors_ref, out_ref):
    block_0 = (gates_ref[0, 0], gates_ref[0, 1])
    block_3 = (gates_ref[1, 0], gates_ref[1, 1])
    columns = []
    for u in range(4):
        parts = []
        for part in range(2):
            start = (u // 2) * 512 + part * 8 + (u % 2) * 4
            tiles = [amps_ref[pl.ds(start + t, 32, stride=16), :] for t in range(4)]
            tiles = swap_bit(swap_bit(tiles, 1, 6), 0, 5)
            parts += tiles
        columns.append(jnp.concatenate(parts, axis=0))
    result = product(mul, block_0, jnp.concatenate(columns, axis=1))
    rows = []
    for u in range(4):
        real = result[:128, u * 128 : (u + 1) * 128]
        imag = result[128:, u * 128 : (u + 1) * 128]
        parts = []
        for value in rotate((factors_ref[0, 0, u], factors_ref[0, 1, u]), real, imag):
            tiles = [value[ah * 32 : (ah + 1) * 32] for ah in range(4)]
            tiles = swap_bit(swap_bit(tiles, 1, 6), 0, 5)
            parts.append(jnp.concatenate(tiles, axis=0))
        rows.append(jnp.concatenate(parts, axis=1))
    result = product(mul_t, block_3, jnp.concatenate(rows, axis=0))
    for u in range(4):
        values = result[:, u * 128 : (u + 1) * 128]
        tiles = [values[ah * 64 : (ah + 1) * 64] for ah in range(4)]
        tiles = swap_bit(swap_bit(tiles, 1, 6), 0, 5)
        for t in range(4):
            out_ref[:, u * 4 + t, :, :] = tiles[t].reshape(8, 8, LANES)


def kernel_c(amps_ref, gates_ref, factors_ref, out_ref):
    block_2 = (gates_ref[2, 0], gates_ref[2, 1])
    block_4 = (gates_ref[3, 0], gates_ref[3, 1])
    columns = []
    for xl in range(4):
        parts = [amps_ref[pl.ds(part * 4 + xl, 128, stride=8), :] for part in range(2)]
        columns.append(jnp.concatenate(parts, axis=0))
    result = product(mul, block_2, jnp.concatenate(columns, axis=1))
    rotated = [
        rotate(
            (factors_ref[1, 0, xl], factors_ref[1, 1, xl]),
            result[:128, xl * 128 : (xl + 1) * 128],
            result[128:, xl * 128 : (xl + 1) * 128],
        )
        for xl in range(4)
    ]
    rows = []
    for gb in range(8):
        for xl in range(4):
            real, imag = rotated[xl]
            rows.append(
                jnp.concatenate(
                    [real[gb * 16 : (gb + 1) * 16], imag[gb * 16 : (gb + 1) * 16]], axis=1
                )
            )
    result = product(mul_t, block_4, jnp.concatenate(rows, axis=0))
    for pair in range(4):
        values = result[:, pair * 128 : (pair + 1) * 128]
        tiles = swap_bit([values[:128], values[128:]], 0, 6)
        for last in range(2):
            gb = pair * 2 + last
            for ah in range(4):
                out_ref[pl.ds(gb * 4 + ah, 32, stride=32), :] = tiles[last][ah * 32 : (ah + 1) * 32]


def kernel_d(amps_ref, gates_ref, out_hbm, out, sems):
    block = (gates_ref[4, 0], gates_ref[4, 1])
    written = []
    for b13 in range(2):
        rows = []
        for b7 in range(2):
            tiles = []
            for xb in range(8):
                start = b7 * 512 + xb * 64 + b13 * 8
                tiles.append(
                    jnp.concatenate(
                        [amps_ref[start + 16 * at : start + 16 * at + 8, :] for at in range(4)], axis=0
                    )
                )
            tiles = swap_bit(swap_bit(swap_bit(tiles, 2, 6), 1, 5), 0, 4)
            for xl in range(4):
                rows.append(jnp.concatenate([tiles[xl], tiles[4 + xl]], axis=1))
        result = product(mul_t, block, jnp.concatenate(rows, axis=0), values_left=True)
        for b7, xl, b11, b8, b12 in itertools.product(range(2), range(4), *[range(2)] * 3):
            at = (b7 * 4 + xl) * 32 + b11 * 16 + b8 * 8 + b12 * 4
            to = b13 * 64 + b12 * 32 + b11 * 16 + xl * 4 + b8 * 2 + b7
            for part in range(2):
                out[pl.ds(2 * to + part, 4, stride=256), :] = result[
                    at : at + 4, part * 128 : (part + 1) * 128
                ]
        for ah in range(4):
            piece = pl.ds(ah * 256 + b13 * 128, 128)
            written.append(
                pltpu.make_async_copy(out.at[piece], out_hbm.at[piece], sems.at[b13 * 4 + ah])
            )
            written[-1].start()
    for copy in written:
        copy.wait()


VMEM = pl.BlockSpec(memory_space=pltpu.VMEM)
HBM = pl.BlockSpec(memory_space=pltpu.HBM)
TABLES = (
    jax.ShapeDtypeStruct((5, 2, 256, 256), BF16),
    jax.ShapeDtypeStruct((2, 2, 4, 128, LANES), F32),
)


def call(kernel, name, out_shape, *operands, space=VMEM, out_space=VMEM, scratch=(), mib=24):
    return pl.pallas_call(
        kernel,
        out_shape=out_shape,
        in_specs=[space] * len(operands),
        out_specs=jax.tree.map(lambda _: out_space, out_shape),
        scratch_shapes=list(scratch),
        compiler_params=pltpu.CompilerParams(vmem_limit_bytes=mib * 1024 * 1024),
        cost_estimate=pl.CostEstimate(flops=400_000_000, bytes_accessed=2_000_000, transcendentals=0),
        name=name,
    )(*operands)


def body(amplitudes, gate_mats, gate_order, phase_pairs, phase_angles):
    pairs = phase_pairs.transpose(0, 2, 1)
    shared = (gate_mats, gate_order, pairs, phase_angles)
    shape = jax.ShapeDtypeStruct((1024, LANES), F32)
    state = amplitudes.reshape(2, 512, LANES).transpose(1, 0, 2).reshape(1024, LANES)
    state = call(
        kernel_a,
        "first_gate",
        jax.ShapeDtypeStruct((64, 16, LANES), F32),
        state,
        *shared,
        space=HBM,
        out_space=HBM,
        mib=63,
        scratch=(
            pltpu.VMEM((1024, LANES), F32),
            pltpu.VMEM((2, 128, LANES), F32),
            pltpu.VMEM((6, 7), jnp.int32),
            pltpu.VMEM((3, 2, 4), jnp.int32),
            pltpu.VMEM((3, 4), F32),
            pltpu.VMEM((64, 16, LANES), F32),
            pltpu.SemaphoreType.DMA((5,)),
            pltpu.SemaphoreType.DMA((4,)),
        ),
    )
    state = exchange(state, ["zh", "y", "zl", "c"]).reshape(1024, LANES)
    gates, factors = call(kernel_tables, "tables", TABLES, *shared)
    state = call(
        kernel_b, "second_gates", jax.ShapeDtypeStruct((8, 16, 8, LANES), F32), state, gates, factors
    )
    state = exchange(state.reshape(1024, LANES), ["x", "c"])
    state = call(kernel_c, "third_gates", shape, state, gates, factors)
    state = exchange(state, ["y", "zl", "c", "zh", "x"])
    state = call(
        kernel_d,
        "last_gate",
        shape,
        state,
        gates,
        out_space=HBM,
        scratch=(pltpu.VMEM((1024, LANES), F32), pltpu.SemaphoreType.DMA((8,))),
    )
    return state.reshape(512, 2, LANES).transpose(1, 0, 2).reshape(2, 65536)


def solution(mesh):
    return jax.shard_map(
        body,
        mesh=mesh,
        in_specs=(P(None, AXES), P(), P(), P(), P()),
        out_specs=P(None, AXES),
        check_vma=False,
    )
```

time: 84.3 us -> 79.5 us (0.943)
  blocking collectives: 71.4 us -> 39.6 us
  waiting for transfers between devices: 0 us -> 15.4 us
  starting transfers between devices: 0 us -> 13.2 us
  local copies, waits for them, and re-layouts: 2.99 us -> 1.14 us
    all_to_all x2 -> x1, blocking collectives: 45.5 us -> 13.6 us  [exchange(): lax.all_to_all(parts, AXES, 0, 0, axis_index_groups=groups, tiled=True)]
    all_to_all x0 -> x1, waiting for transfers between devices: none -> 15.4 us  [exchange(): lax.all_to_all(parts, AXES, 0, 0, axis_index_groups=groups, tiled=True)]
    all_to_all x0 -> x1, starting transfers between devices: none -> 13.2 us  [exchange(): lax.all_to_all(parts, AXES, 0, 0, axis_index_groups=groups, tiled=True)]
    unnamed x11 -> x8, local copies, waits for them, and re-layouts: 2.99 us -> 1.14 us
    pallas_call x4 -> x5, Pallas kernels: 9.56 us -> 9.92 us  [call(): pl.pallas_call(kernel, out_shape=out_shape, in_specs=[space] * len(operan...]
  transfers between devices with their start and end apart: 0 -> 1, of which waited for: 0 -> 1; matrix products, arithmetic and copies ran while one was open for 0% -> 0% of each run, Pallas kernels for 0% -> 3%
where the time goes in v1:
time: 79.5 us; the launch traced here: 79.2 us
  blocking collectives  39.6 us (50%)
  waiting for transfers between devices  15.4 us (19%)
  starting transfers between devices  13.2 us (17%)
  Pallas kernels  9.92 us (12%)
  local copies, waits for them, and re-layouts  1.14 us (1%)
    all_to_all x1, blocking collectives, exchange(): moved = lax.all_to_all(parts, AXES, 0, 0, tiled=True)  26 us
    all_to_all x1, waiting for transfers between devices, exchange(): lax.all_to_all(parts, AXES, 0, 0, axis_index_groups=groups, tiled=True)  15.4 us
    all_to_all x1, blocking collectives, exchange(): lax.all_to_all(parts, AXES, 0, 0, axis_index_groups=groups, tiled=True)  13.6 us
    all_to_all x1, starting transfers between devices, exchange(): lax.all_to_all(parts, AXES, 0, 0, axis_index_groups=groups, tiled=True)  13.2 us
    pallas_call x5, Pallas kernels, call(): pl.pallas_call(kernel, out_shape=out_shape, in_specs=[space] * len(operan...  9.92 us
  transfers between devices with their start and end apart: 1, of which 1 were waited for; matrix products, arithmetic and copies ran while one was open for 0% of the time, Pallas kernels for 3%

profile of v1, /device:TPU:1, one launch (start us, length us, event | category | flops | bytes accessed | tf_op | source)
XLA Modules:
  0.0 79.2 jit_solution(7046709335223966142)
XLA Ops:
  0.0 0.0 copy-start.1
  0.0 0.0 copy-start.2
  0.0 0.0 copy-start.3
  0.0 3.0 %first_gate.1 = f32[64,16,128]{2,1,0:T(8,128)} custom-call(f32[1024,128]{1,0:T(8,128)} %bitcast.23, f32[6,2,128,128]{3,2,1,0:T(8,128)} %mats_ref.1, s32[6,7]{1,0:T(8,128)} %order_ref.1, s32[3,2,4]{2,1,0:T(2,128)} %bitcast.21, f32[3,4]{1,0:T(4,128)} %angles_ref.1), custom_call_target="tpu_custom_call" | custom-call | flops 400000000 | bytes 2000000 | tf_op jit(solution)/shard_map/first_gate/pallas_call | solution.py:349
  3.1 13.2 %all-to-all-start = ((f32[64,16,128]{2,1,0:T(8,128)}), f32[64,16,128]{2,1,0:T(8,128)S(1)}, u32[]{:S(2)}, u32[]{:S(2)}) async-start(f32[64,16,128]{2,1,0:T(8,128)} %first_gate.1), calls=%async_computation | async-start | bytes 1048576 | tf_op jit(solution)/shard_map/all_to_all | solution.py:35
  16.2 0.0 copy-done.1
  16.3 0.0 copy-done.2
  16.3 0.0 copy-done.3
  16.3 0.0 copy-start
  16.3 1.1 %copy-done = f32[6,2,128,128]{3,2,1,0:T(8,128)S(1)} copy-done((f32[6,2,128,128]{3,2,1,0:T(8,128)S(1)}, f32[6,2,128,128]{3,2,1,0:T(8,128)}, u32[]{:S(2)}) %copy-start) | copy-done | bytes 786456
  17.4 2.2 %tables.1 = (bf16[5,2,256,256]{3,2,1,0:T(8,128)(2,1)S(1)}, f32[2,2,4,128,128]{4,3,2,1,0:T(8,128)S(1)}) custom-call(f32[6,2,128,128]{3,2,1,0:T(8,128)S(1)} %copy-done, s32[6,7]{1,0:T(8,128)S(1)} %copy-done.1, s32[3,2,4]{2,1,0:T(2,128)S(1)} %bitcast.22, f32[3,4]{1,0:T(4,128)S(1)} %copy-done.3), custom_call_target="tpu_custom_call" | custom-call | flops 400000000 | bytes 2000000 | tf_op jit(solution)/shard_map/tables/pallas_call | solution.py:349
  19.7 15.4 %all-to-all-done = f32[64,16,128]{2,1,0:T(8,128)S(1)} async-done(((f32[64,16,128]{2,1,0:T(8,128)}), f32[64,16,128]{2,1,0:T(8,128)S(1)}, u32[]{:S(2)}, u32[]{:S(2)}) %all-to-all-start) | async-done | bytes 524320 | tf_op jit(solution)/shard_map/all_to_all | solution.py:35
  35.1 1.7 %second_gates.1 = f32[8,16,8,128]{3,2,1,0:T(8,128)S(1)} custom-call(f32[1024,128]{1,0:T(8,128)S(1)} %bitcast.16, bf16[5,2,256,256]{3,2,1,0:T(8,128)(2,1)S(1)} %get-tuple-element.7.gates_ref, f32[2,2,4,128,128]{4,3,2,1,0:T(8,128)S(1)} %get-tuple-element.8.factors_ref), custom_call_target="tpu_custom_call" | custom-call | flops 400000000 | bytes 2000000 | tf_op jit(solution)/shard_map/second_gates/pallas_call | solution.py:349
  36.7 13.6 %all_to_all.15 = f32[8,128,128]{2,1,0:T(8,128)S(1)} all-to-all(f32[8,128,128]{2,1,0:T(8,128)S(1)} %bitcast.20), channel_id=1, replica_groups={{0,8,1,9,2,10,3,11},{4,12,5,13,6,14,7,15},{16,24,17,25,18,26,19,27},{20..., dimensions={0} | all-to-all | bytes 1048576 | tf_op jit(solution)/shard_map/all_to_all | solution.py:35
  50.3 1.2 %third_gates.1 = f32[1024,128]{1,0:T(8,128)S(1)} custom-call(f32[1024,128]{1,0:T(8,128)S(1)} %bitcast.17, bf16[5,2,256,256]{3,2,1,0:T(8,128)(2,1)S(1)} %get-tuple-element.7.gates_ref, f32[2,2,4,128,128]{4,3,2,1,0:T(8,128)S(1)} %get-tuple-element.8.factors_ref), custom_call_target="tpu_custom_call" | custom-call | flops 400000000 | bytes 2000000 | tf_op jit(solution)/shard_map/third_gates/pallas_call | solution.py:349
  51.5 26.0 %all_to_all.16 = f32[256,4,128]{2,1,0:T(4,128)S(1)} all-to-all(f32[256,4,128]{2,1,0:T(4,128)S(1)} %bitcast.18), channel_id=1, replica_groups=mesh['qa'=32,'qb'=8] {'qa','qb'}, dimensions={0} | all-to-all | bytes 1048576 | tf_op jit(solution)/shard_map/all_to_all | solution.py:33
  77.5 1.7 %last_gate.1 = f32[1024,128]{1,0:T(8,128)} custom-call(f32[1024,128]{1,0:T(8,128)S(1)} %bitcast.19, bf16[5,2,256,256]{3,2,1,0:T(8,128)(2,1)S(1)} %get-tuple-element.7.gates_ref), custom_call_target="tpu_custom_call" | custom-call | flops 400000000 | bytes 2000000 | tf_op jit(solution)/shard_map/last_gate/pallas_call | solution.py:349
Async XLA Ops:
  0.0 16.2 %copy-start.1 = (s32[6,7]{1,0:T(8,128)S(1)}, s32[6,7]{1,0:T(8,128)}, u32[]{:S(2)}) copy-start(s32[6,7]{1,0:T(8,128)} %order_ref.1) | copy-start | bytes 508
  0.0 16.3 %copy-start.2 = (s32[3,4,2]{1,2,0:T(2,128)S(1)}, s32[3,4,2]{1,2,0:T(2,128)}, u32[]{:S(2)}) copy-start(s32[3,4,2]{1,2,0:T(2,128)} %param.8) | copy-start | bytes 292
  0.0 16.3 %copy-start.3 = (f32[3,4]{1,0:T(4,128)S(1)}, f32[3,4]{1,0:T(4,128)}, u32[]{:S(2)}) copy-start(f32[3,4]{1,0:T(4,128)} %angles_ref.1) | copy-start | bytes 148
  3.1 32.0 %all-to-all-start = ((f32[64,16,128]{2,1,0:T(8,128)}), f32[64,16,128]{2,1,0:T(8,128)S(1)}, u32[]{:S(2)}, u32[]{:S(2)}) async-start(f32[64,16,128]{2,1,0:T(8,128)} %first_gate.1), calls=%async_computation | async-start | bytes 1048576 | tf_op jit(solution)/shard_map/all_to_all | solution.py:35
  16.3 1.1 %copy-start = (f32[6,2,128,128]{3,2,1,0:T(8,128)S(1)}, f32[6,2,128,128]{3,2,1,0:T(8,128)}, u32[]{:S(2)}) copy-start(f32[6,2,128,128]{3,2,1,0:T(8,128)} %mats_ref.1) | copy-start | bytes 2359300

commit v2 on v1

--- a/solution.py
+++ b/solution.py
@@ -34,6 +34,13 @@
     else:
         moved = lax.all_to_all(parts, AXES, 0, 0, axis_index_groups=groups, tiled=True)
     return moved.reshape(values.shape)
+
+
+def from_partner(value, varying, mask):
+    pairs = [
+        (group[at], group[at ^ mask]) for group in device_groups([varying]) for at in range(len(group))
+    ]
+    return lax.ppermute(value, AXES, pairs)
 
 
 def iota(axis, shape=(128, 128)):
@@ -151,6 +158,11 @@
         if other == number:
             continue
         first, second = tiles[number], tiles[other]
+        if 2 * width == LANES:
+            moved = pltpu.roll(jnp.where(low, second, first), width, 1)
+            out[number] = jnp.where(low, first, moved)
+            out[other] = jnp.where(low, moved, second)
+            continue
         out[number] = jnp.where(low, first, pltpu.roll(second, width, 1))
         out[other] = jnp.where(low, pltpu.roll(first, LANES - width, 1), second)
     return out
@@ -218,8 +230,8 @@
     natural = iota(0)
     arrived = take_bits(natural, (0, 1, 2, 6, 3, 4, 5))
     for slot, gate in enumerate((0, 3, 2, 4, 5)):
-        rows = natural
-        columns = arrived if gate == 2 else natural
+        rows = natural ^ (x * 8 + core * 4) if gate == 3 else natural
+        columns = arrived ^ (x * 16 + core * 8) if gate == 2 else natural
         blocks = gate_block(
             mats_ref.at[gate], order_ref, gate, rows, None if rows is columns else columns
         )
@@ -235,7 +247,7 @@
                 gates_ref[slot, half] = block
 
 
-def kernel_b(amps_ref, gates_ref, factors_ref, out_ref):
+def kernel_b(amps_ref, gates_ref, factors_ref, kept_ref, sent_ref):
     block_0 = (gates_ref[0, 0], gates_ref[0, 1])
     block_3 = (gates_ref[1, 0], gates_ref[1, 1])
     columns = []
@@ -264,15 +276,24 @@
         tiles = [values[ah * 64 : (ah + 1) * 64] for ah in range(4)]
         tiles = swap_bit(swap_bit(tiles, 1, 6), 0, 5)
         for t in range(4):
-            out_ref[:, u * 4 + t, :, :] = tiles[t].reshape(8, 8, LANES)
-
-
-def kernel_c(amps_ref, gates_ref, factors_ref, out_ref):
+            to = (u * 4 + t) * 8
+            for k in range(4):
+                kept_ref[k, to : to + 8, :] = tiles[t][k * 16 : k * 16 + 8]
+                sent_ref[k, to : to + 8, :] = tiles[t][k * 16 + 8 : k * 16 + 16]
+
+
+def kernel_c(kept_ref, got_ref, *refs):
+    arrived, (gates_ref, factors_ref, out_ref) = refs[:3], refs[3:]
     block_2 = (gates_ref[2, 0], gates_ref[2, 1])
     block_4 = (gates_ref[3, 0], gates_ref[3, 1])
     columns = []
     for xl in range(4):
-        parts = [amps_ref[pl.ds(part * 4 + xl, 128, stride=8), :] for part in range(2)]
+        parts = []
+        for part in range(2):
+            rows = pl.ds(part * 4 + xl, 16, stride=8)
+            parts += [kept_ref[0, rows, :], got_ref[0, rows, :]]
+            for ref in (arrived[2], arrived[0], arrived[1]):
+                parts += [ref[0, rows, :], ref[1, rows, :]]
         columns.append(jnp.concatenate(parts, axis=0))
     result = product(mul, block_2, jnp.concatenate(columns, axis=1))
     rotated = [
@@ -385,11 +406,13 @@
     )
     state = exchange(state, ["zh", "y", "zl", "c"]).reshape(1024, LANES)
     gates, factors = call(kernel_tables, "tables", TABLES, *shared)
+    half = jax.ShapeDtypeStruct((4, 128, LANES), F32)
+    kept, sent = call(kernel_b, "second_gates", (half, half), state, gates, factors)
+    got = from_partner(sent, "c", 1)
+    arrived = {k: from_partner(jnp.stack([kept[k], got[k]]), "x", k) for k in (2, 3, 1)}
     state = call(
-        kernel_b, "second_gates", jax.ShapeDtypeStruct((8, 16, 8, LANES), F32), state, gates, factors
+        kernel_c, "third_gates", shape, kept, got, arrived[2], arrived[3], arrived[1], gates, factors
     )
-    state = exchange(state.reshape(1024, LANES), ["x", "c"])
-    state = call(kernel_c, "third_gates", shape, state, gates, factors)
     state = exchange(state, ["y", "zl", "c", "zh", "x"])
     state = call(
         kernel_d,

time: 79.5 us -> 78 us (0.981)
  blocking collectives: 39.6 us -> 27.2 us
  waiting for transfers between devices: 15.4 us -> 22.3 us
  starting transfers between devices: 13.2 us -> 17.1 us
    all_to_all x1 -> x0, blocking collectives: 13.6 us -> none  [exchange(): lax.all_to_all(parts, AXES, 0, 0, axis_index_groups=groups, tiled=True)]
    ppermute x0 -> x4, waiting for transfers between devices: none -> 6.96 us  [from_partner(): return lax.ppermute(value, AXES, pairs)]
    ppermute x0 -> x4, starting transfers between devices: none -> 3.96 us  [from_partner(): return lax.ppermute(value, AXES, pairs)]
    all_to_all x1, blocking collectives: 26 us -> 27.2 us  [exchange(): moved = lax.all_to_all(parts, AXES, 0, 0, tiled=True)]
  transfers between devices with their start and end apart: 1 -> 5, of which waited for: 1 -> 5; matrix products, arithmetic and copies ran while one was open for 0% -> 0% of each run, Pallas kernels for 3% -> 3%
where the time goes in v2:
time: 78 us; the launch traced here: 77.7 us
  blocking collectives  27.2 us (35%)
  waiting for transfers between devices  22.3 us (29%)
  starting transfers between devices  17.1 us (22%)
  Pallas kernels  9.76 us (13%)
  local copies, waits for them, and re-layouts  1.17 us (2%)
    all_to_all x1, blocking collectives, exchange(): moved = lax.all_to_all(parts, AXES, 0, 0, tiled=True)  27.2 us
    all_to_all x1, waiting for transfers between devices, exchange(): lax.all_to_all(parts, AXES, 0, 0, axis_index_groups=groups, tiled=True)  15.4 us
    all_to_all x1, starting transfers between devices, exchange(): lax.all_to_all(parts, AXES, 0, 0, axis_index_groups=groups, tiled=True)  13.2 us
    pallas_call x5, Pallas kernels, call(): pl.pallas_call(kernel, out_shape=out_shape, in_specs=[space] * len(operan...  9.76 us
    ppermute x4, waiting for transfers between devices, from_partner(): return lax.ppermute(value, AXES, pairs)  6.96 us
    ppermute x4, starting transfers between devices, from_partner(): return lax.ppermute(value, AXES, pairs)  3.96 us
  transfers between devices with their start and end apart: 5, of which 5 were waited for; matrix products, arithmetic and copies ran while one was open for 0% of the time, Pallas kernels for 3%

profile of v2, /device:TPU:1, one launch (start us, length us, event | category | flops | bytes accessed | tf_op | source)
XLA Modules:
  0.0 77.7 jit_solution(2099268458944330046)
XLA Ops:
  0.0 0.0 copy-start.1
  0.0 0.0 copy-start.2
  0.0 0.0 copy-start.3
  0.0 3.0 %first_gate.1 = f32[64,16,128]{2,1,0:T(8,128)} custom-call(f32[1024,128]{1,0:T(8,128)} %bitcast.19, f32[6,2,128,128]{3,2,1,0:T(8,128)} %mats_ref.1, s32[6,7]{1,0:T(8,128)} %order_ref.1, s32[3,2,4]{2,1,0:T(2,128)} %bitcast.17, f32[3,4]{1,0:T(4,128)} %angles_ref.1), custom_call_target="tpu_custom_call" | custom-call | flops 400000000 | bytes 2000000 | tf_op jit(solution)/shard_map/first_gate/pallas_call | solution.py:370
  3.1 13.2 %all-to-all-start = ((f32[64,16,128]{2,1,0:T(8,128)}), f32[64,16,128]{2,1,0:T(8,128)S(1)}, u32[]{:S(2)}, u32[]{:S(2)}) async-start(f32[64,16,128]{2,1,0:T(8,128)} %first_gate.1), calls=%async_computation | async-start | bytes 1048576 | tf_op jit(solution)/shard_map/all_to_all | solution.py:35
  16.2 0.0 copy-done.1
  16.3 0.0 copy-done.2
  16.3 0.0 copy-done.3
  16.3 0.0 copy-start
  16.3 1.1 %copy-done = f32[6,2,128,128]{3,2,1,0:T(8,128)S(1)} copy-done((f32[6,2,128,128]{3,2,1,0:T(8,128)S(1)}, f32[6,2,128,128]{3,2,1,0:T(8,128)}, u32[]{:S(2)}) %copy-start) | copy-done | bytes 786456
  17.4 2.2 %tables.1 = (bf16[5,2,256,256]{3,2,1,0:T(8,128)(2,1)S(1)}, f32[2,2,4,128,128]{4,3,2,1,0:T(8,128)S(1)}) custom-call(f32[6,2,128,128]{3,2,1,0:T(8,128)S(1)} %copy-done, s32[6,7]{1,0:T(8,128)S(1)} %copy-done.1, s32[3,2,4]{2,1,0:T(2,128)S(1)} %bitcast.18, f32[3,4]{1,0:T(4,128)S(1)} %copy-done.3), custom_call_target="tpu_custom_call" | custom-call | flops 400000000 | bytes 2000000 | tf_op jit(solution)/shard_map/tables/pallas_call | solution.py:370
  19.7 15.4 %all-to-all-done = f32[64,16,128]{2,1,0:T(8,128)S(1)} async-done(((f32[64,16,128]{2,1,0:T(8,128)}), f32[64,16,128]{2,1,0:T(8,128)S(1)}, u32[]{:S(2)}, u32[]{:S(2)}) %all-to-all-start) | async-done | bytes 524320 | tf_op jit(solution)/shard_map/all_to_all | solution.py:35
  35.1 1.6 %second_gates.1 = (f32[4,128,128]{2,1,0:T(8,128)S(1)}, f32[4,128,128]{2,1,0:T(8,128)S(1)}) custom-call(f32[1024,128]{1,0:T(8,128)S(1)} %bitcast.14, bf16[5,2,256,256]{3,2,1,0:T(8,128)(2,1)S(1)} %get-tuple-element.9.gates_ref.refs_3_, f32[2,2,4,128,128]{4,3,2,1,0:T(8,128)S(1)} %get-tuple-element.10.factors_ref.refs_4_), custom_call_target="tpu_custom_call" | custom-call | flops 400000000 | bytes 2000000 | tf_op jit(solution)/shard_map/second_gates/pallas_call | solution.py:370
  36.6 0.1 collective-permute-start
  36.7 1.5 %collective-permute-done.got_ref = f32[4,128,128]{2,1,0:T(8,128)S(1)} collective-permute-done((f32[4,128,128]{2,1,0:T(8,128)S(1)}, f32[4,128,128]{2,1,0:T(8,128)S(1)}, u32[]{:S(2)}, u32[]{:S(2)}) %collective-permute-start) | collective-permute-done | bytes 262176 | tf_op jit(solution)/shard_map/ppermute | solution.py:43
  38.3 2.8 %collective-permute-start.1 = (f32[2,128,128]{2,1,0:T(8,128)S(1)}, f32[2,128,128]{2,1,0:T(8,128)S(1)}, u32[]{:S(2)}, u32[]{:S(2)}) collective-permute-start(f32[2,128,128]{2,1,0:T(8,128)S(1)} %pad_maximum_fusion), channel_id=1, source_target_pairs={{0,2},{1,3},{2,0},{3,1},{4,6},{5,7},{6,4},{7,5},{8,10},{9,11},{10,... | collective-permute-start | bytes 393224 | tf_op jit(solution)/shard_map/ppermute | solution.py:43
  41.1 0.9 %collective-permute-start.2 = (f32[2,128,128]{2,1,0:T(8,128)S(1)}, f32[2,128,128]{2,1,0:T(8,128)S(1)}, u32[]{:S(2)}, u32[]{:S(2)}) collective-permute-start(f32[2,128,128]{2,1,0:T(8,128)S(1)} %pad_maximum_fusion.1), channel_id=1, source_target_pairs={{0,3},{1,2},{2,1},{3,0},{4,7},{5,6},{6,5},{7,4},{8,11},{9,10},{10,... | collective-permute-start | bytes 393224 | tf_op jit(solution)/shard_map/ppermute | solution.py:43
  42.1 0.1 collective-permute-start.3
  42.2 2.6 %collective-permute-done.1.refs_0_ = f32[2,128,128]{2,1,0:T(8,128)S(1)} collective-permute-done((f32[2,128,128]{2,1,0:T(8,128)S(1)}, f32[2,128,128]{2,1,0:T(8,128)S(1)}, u32[]{:S(2)}, u32[]{:S(2)}) %collective-permute-start.1) | collective-permute-done | bytes 131104 | tf_op jit(solution)/shard_map/ppermute | solution.py:43
  44.8 2.8 %collective-permute-done.2.refs_1_ = f32[2,128,128]{2,1,0:T(8,128)S(1)} collective-permute-done((f32[2,128,128]{2,1,0:T(8,128)S(1)}, f32[2,128,128]{2,1,0:T(8,128)S(1)}, u32[]{:S(2)}, u32[]{:S(2)}) %collective-permute-start.2) | collective-permute-done | bytes 131104 | tf_op jit(solution)/shard_map/ppermute | solution.py:43
  47.6 0.1 collective-permute-done.3.refs_2_
  47.6 1.2 %third_gates.1 = f32[1024,128]{1,0:T(8,128)S(1)} custom-call(f32[4,128,128]{2,1,0:T(8,128)S(1)} %get-tuple-element.11.kept_ref, f32[4,128,128]{2,1,0:T(8,128)S(1)} %collective-permute-done.got_ref, f32[2,128,128]{2,1,0:T(8,128)S(1)} %collective-permute-done.1.refs_0_, f32[2,128,128]{2,1,0:T(8,128)S(1)} %collective-permute-done.2.refs_1_, ...), custom_call_target="tpu_custom_call" | custom-call | flops 400000000 | bytes 2000000 | tf_op jit(solution)/shard_map/third_gates/pallas_call | solution.py:370
  48.8 27.2 %all_to_all.10 = f32[256,4,128]{2,1,0:T(4,128)S(1)} all-to-all(f32[256,4,128]{2,1,0:T(4,128)S(1)} %bitcast.16), channel_id=1, replica_groups=mesh['qa'=32,'qb'=8] {'qa','qb'}, dimensions={0} | all-to-all | bytes 1048576 | tf_op jit(solution)/shard_map/all_to_all | solution.py:33
  76.0 1.7 %last_gate.1 = f32[1024,128]{1,0:T(8,128)} custom-call(f32[1024,128]{1,0:T(8,128)S(1)} %bitcast.15, bf16[5,2,256,256]{3,2,1,0:T(8,128)(2,1)S(1)} %get-tuple-element.9.gates_ref.refs_3_), custom_call_target="tpu_custom_call" | custom-call | flops 400000000 | bytes 2000000 | tf_op jit(solution)/shard_map/last_gate/pallas_call | solution.py:370
  (5 shorter events, 0.1 us)
Async XLA Ops:
  0.0 16.2 %copy-start.1 = (s32[6,7]{1,0:T(8,128)S(1)}, s32[6,7]{1,0:T(8,128)}, u32[]{:S(2)}) copy-start(s32[6,7]{1,0:T(8,128)} %order_ref.1) | copy-start | bytes 508
  0.0 16.3 %copy-start.2 = (s32[3,4,2]{1,2,0:T(2,128)S(1)}, s32[3,4,2]{1,2,0:T(2,128)}, u32[]{:S(2)}) copy-start(s32[3,4,2]{1,2,0:T(2,128)} %param.8) | copy-start | bytes 292
  0.0 16.3 %copy-start.3 = (f32[3,4]{1,0:T(4,128)S(1)}, f32[3,4]{1,0:T(4,128)}, u32[]{:S(2)}) copy-start(f32[3,4]{1,0:T(4,128)} %angles_ref.1) | copy-start | bytes 148
  3.1 32.0 %all-to-all-start = ((f32[64,16,128]{2,1,0:T(8,128)}), f32[64,16,128]{2,1,0:T(8,128)S(1)}, u32[]{:S(2)}, u32[]{:S(2)}) async-start(f32[64,16,128]{2,1,0:T(8,128)} %first_gate.1), calls=%async_computation | async-start | bytes 1048576 | tf_op jit(solution)/shard_map/all_to_all | solution.py:35
  16.3 1.1 %copy-start = (f32[6,2,128,128]{3,2,1,0:T(8,128)S(1)}, f32[6,2,128,128]{3,2,1,0:T(8,128)}, u32[]{:S(2)}) copy-start(f32[6,2,128,128]{3,2,1,0:T(8,128)} %mats_ref.1) | copy-start | bytes 2359300
  36.6 1.6 %collective-permute-start = (f32[4,128,128]{2,1,0:T(8,128)S(1)}, f32[4,128,128]{2,1,0:T(8,128)S(1)}, u32[]{:S(2)}, u32[]{:S(2)}) collective-permute-start(f32[4,128,128]{2,1,0:T(8,128)S(1)} %get-tuple-element.12), channel_id=1, source_target_pairs={{0,8},{8,0},{1,9},{9,1},{2,10},{10,2},{3,11},{11,3},{4,12},{12,4},... | collective-permute-start | bytes 786440 | tf_op jit(solution)/shard_map/ppermute | solution.py:43
  38.3 6.5 %collective-permute-start.1 = (f32[2,128,128]{2,1,0:T(8,128)S(1)}, f32[2,128,128]{2,1,0:T(8,128)S(1)}, u32[]{:S(2)}, u32[]{:S(2)}) collective-permute-start(f32[2,128,128]{2,1,0:T(8,128)S(1)} %pad_maximum_fusion), channel_id=1, source_target_pairs={{0,2},{1,3},{2,0},{3,1},{4,6},{5,7},{6,4},{7,5},{8,10},{9,11},{10,... | collective-permute-start | bytes 393224 | tf_op jit(solution)/shard_map/ppermute | solution.py:43
  41.1 6.5 %collective-permute-start.2 = (f32[2,128,128]{2,1,0:T(8,128)S(1)}, f32[2,128,128]{2,1,0:T(8,128)S(1)}, u32[]{:S(2)}, u32[]{:S(2)}) collective-permute-start(f32[2,128,128]{2,1,0:T(8,128)S(1)} %pad_maximum_fusion.1), channel_id=1, source_target_pairs={{0,3},{1,2},{2,1},{3,0},{4,7},{5,6},{6,5},{7,4},{8,11},{9,10},{10,... | collective-permute-start | bytes 393224 | tf_op jit(solution)/shard_map/ppermute | solution.py:43
  42.1 5.6 %collective-permute-start.3 = (f32[2,128,128]{2,1,0:T(8,128)S(1)}, f32[2,128,128]{2,1,0:T(8,128)S(1)}, u32[]{:S(2)}, u32[]{:S(2)}) collective-permute-start(f32[2,128,128]{2,1,0:T(8,128)S(1)} %pad_maximum_fusion.2), channel_id=1, source_target_pairs={{0,1},{1,0},{2,3},{3,2},{4,5},{5,4},{6,7},{7,6},{8,9},{9,8},{10,11... | collective-permute-start | bytes 393224 | tf_op jit(solution)/shard_map/ppermute | solution.py:43

commit v3 on v2

--- a/solution.py
+++ b/solution.py
@@ -29,10 +29,7 @@
 def exchange(values, varying):
     groups = device_groups(varying)
     parts = values.reshape(len(groups[0]), -1, LANES)
-    if len(groups) == 1:
-        moved = lax.all_to_all(parts, AXES, 0, 0, tiled=True)
-    else:
-        moved = lax.all_to_all(parts, AXES, 0, 0, axis_index_groups=groups, tiled=True)
+    moved = lax.all_to_all(parts, AXES, 0, 0, axis_index_groups=groups, tiled=True)
     return moved.reshape(values.shape)
 
 
@@ -99,12 +96,14 @@
     return out
 
 
+def thrice(high, low):
+    return jnp.concatenate([high, high, low], axis=1)
+
+
 def product(multiply, block, values, values_left=False):
     high, low = halves(values)
-    block_high, block_low = block
-    if values_left:
-        return multiply(high, block_high) + (multiply(low, block_high) + multiply(high, block_low))
-    return multiply(block_high, high) + (multiply(block_high, low) + multiply(block_low, high))
+    values = jnp.concatenate([high, low, high], axis=0 if multiply is mul else 1)
+    return multiply(values, block) if values_left else multiply(block, values)
 
 
 def sign_of(index, pairs, layer, term):
@@ -171,7 +170,7 @@
 def place():
     qa = lax.axis_index("qa")
     qb = lax.axis_index("qb")
-    return qa // 2, qa % 2, qb // 4, qb % 4
+    return qa // 8, qa // 2 % 4, qa % 2, qb // 4, qb % 4
 
 
 def kernel_a(
@@ -188,9 +187,9 @@
         copy.start()
     for copy in copies[:4]:
         copy.wait()
-    block = full_block(gate_block(mats, order, 1))
-    yz, core, zh, x = place()
-    device = yz * (1 << 20) + core * (1 << 19) + zh * (1 << 18) + x * (1 << 16)
+    block = thrice(*full_block(gate_block(mats, order, 1)))
+    y, zl, core, zh, x = place()
+    device = y * (1 << 22) + zl * (1 << 20) + core * (1 << 19) + zh * (1 << 18) + x * (1 << 16)
     phase = Phase(pairs, angles, 0, iota(0) * 512 + iota(1))
     copies[4].wait()
     written = []
@@ -211,149 +210,148 @@
 
 
 def kernel_tables(mats_ref, order_ref, pairs_ref, angles_ref, gates_ref, factors_ref):
-    yz, core, zh, x = place()
+    y, zl, core, zh, x = place()
+    held = y * (1 << 7) + zh * (1 << 6) + zl * (1 << 4)
     row, lane = iota(0), iota(1)
     index = (row // 32) * (1 << 14) + (row % 32) * (1 << 19) + (lane // 32) + (lane % 32) * 512
     phase = Phase(pairs_ref, angles_ref, 1, index)
-    device = yz * (1 << 4) + core * (1 << 3) + zh * (1 << 8) + x * (1 << 16)
+    device = held + core * (1 << 3) + x * (1 << 16)
     for u in range(4):
         factor = phase.factor(device + (u // 2) * (1 << 18) + (u % 2) * 4)
         for part in range(2):
             factors_ref[0, part, u] = factor[part]
     index = (row // 16) * (1 << 16) + (row % 16) + (lane // 32) * (1 << 14) + (lane % 32) * (1 << 19)
     phase = Phase(pairs_ref, angles_ref, 2, index)
-    device = yz * (1 << 4) + core * (1 << 11) + zh * (1 << 8) + x * (1 << 12)
+    device = held + core * (1 << 13) + x * (1 << 11)
     for xl in range(4):
         factor = phase.factor(device + xl * 512)
         for part in range(2):
             factors_ref[1, part, xl] = factor[part]
     natural = iota(0)
     arrived = take_bits(natural, (0, 1, 2, 6, 3, 4, 5))
+    leaving = take_bits(natural, (0, 3, 4, 1, 2, 5, 6))
     for slot, gate in enumerate((0, 3, 2, 4, 5)):
-        rows = natural ^ (x * 8 + core * 4) if gate == 3 else natural
-        columns = arrived ^ (x * 16 + core * 8) if gate == 2 else natural
+        rows = columns = natural
+        if gate == 3:
+            rows = natural ^ (core * 16 + x * 4)
+        if gate == 2:
+            columns = arrived ^ (x * 16 + core * 8)
+        if gate == 4:
+            rows = leaving
         blocks = gate_block(
             mats_ref.at[gate], order_ref, gate, rows, None if rows is columns else columns
         )
+        block = thrice(*full_block(blocks))
         if gate == 3:
-            for half, (vr, vi) in enumerate(blocks):
-                vr, vi = vr.astype(F32), vi.astype(F32)
-                top = jnp.concatenate([vr, -vi], axis=1).reshape(32, 4, 256)
-                bottom = jnp.concatenate([vi, vr], axis=1).reshape(32, 4, 256)
-                mixed = jnp.concatenate([top, bottom], axis=1).reshape(256, 256)
-                gates_ref[slot, half] = mixed.astype(BF16)
-        else:
-            for half, block in enumerate(full_block(blocks)):
-                gates_ref[slot, half] = block
-
-
-def kernel_b(amps_ref, gates_ref, factors_ref, kept_ref, sent_ref):
-    block_0 = (gates_ref[0, 0], gates_ref[0, 1])
-    block_3 = (gates_ref[1, 0], gates_ref[1, 1])
-    columns = []
-    for u in range(4):
-        parts = []
-        for part in range(2):
-            start = (u // 2) * 512 + part * 8 + (u % 2) * 4
-            tiles = [amps_ref[pl.ds(start + t, 32, stride=16), :] for t in range(4)]
+            block = block.astype(F32).reshape(2, 32, 4, 768)
+            block = jnp.concatenate([block[0], block[1]], axis=1).reshape(256, 768).astype(BF16)
+        gates_ref[slot] = block
+
+
+def kernel_b(amps_ref, gates_ref, factors_ref, kept_ref, soon_ref, later_ref):
+    for first in range(0, 4, 2):
+        group = range(first, first + 2)
+        columns = []
+        for u in group:
+            parts = []
+            for part in range(2):
+                start = (u // 2) * 128 + part * 8 + (u % 2) * 4
+                tiles = [
+                    jnp.concatenate(
+                        [amps_ref[pl.ds(y * 256 + start + t, 8, stride=16), :] for y in range(4)], axis=0
+                    )
+                    for t in range(4)
+                ]
+                tiles = swap_bit(swap_bit(tiles, 1, 6), 0, 5)
+                parts += tiles
+            columns.append(jnp.concatenate(parts, axis=0))
+        result = product(mul, gates_ref[0], jnp.concatenate(columns, axis=1))
+        rows = []
+        for at, u in enumerate(group):
+            real = result[:128, at * 128 : (at + 1) * 128]
+            imag = result[128:, at * 128 : (at + 1) * 128]
+            parts = []
+            for value in rotate((factors_ref[0, 0, u], factors_ref[0, 1, u]), real, imag):
+                tiles = [value[ah * 32 : (ah + 1) * 32] for ah in range(4)]
+                tiles = swap_bit(swap_bit(tiles, 1, 6), 0, 5)
+                parts.append(jnp.concatenate(tiles, axis=0))
+            rows.append(jnp.concatenate(parts, axis=1))
+        result = product(mul_t, gates_ref[1], jnp.concatenate(rows, axis=0))
+        for at, u in enumerate(group):
+            values = result[:, at * 128 : (at + 1) * 128]
+            tiles = [values[ah * 64 : (ah + 1) * 64] for ah in range(4)]
             tiles = swap_bit(swap_bit(tiles, 1, 6), 0, 5)
-            parts += tiles
-        columns.append(jnp.concatenate(parts, axis=0))
-    result = product(mul, block_0, jnp.concatenate(columns, axis=1))
-    rows = []
-    for u in range(4):
-        real = result[:128, u * 128 : (u + 1) * 128]
-        imag = result[128:, u * 128 : (u + 1) * 128]
-        parts = []
-        for value in rotate((factors_ref[0, 0, u], factors_ref[0, 1, u]), real, imag):
-            tiles = [value[ah * 32 : (ah + 1) * 32] for ah in range(4)]
-            tiles = swap_bit(swap_bit(tiles, 1, 6), 0, 5)
-            parts.append(jnp.concatenate(tiles, axis=0))
-        rows.append(jnp.concatenate(parts, axis=1))
-    result = product(mul_t, block_3, jnp.concatenate(rows, axis=0))
-    for u in range(4):
-        values = result[:, u * 128 : (u + 1) * 128]
-        tiles = [values[ah * 64 : (ah + 1) * 64] for ah in range(4)]
-        tiles = swap_bit(swap_bit(tiles, 1, 6), 0, 5)
-        for t in range(4):
-            to = (u * 4 + t) * 8
-            for k in range(4):
-                kept_ref[k, to : to + 8, :] = tiles[t][k * 16 : k * 16 + 8]
-                sent_ref[k, to : to + 8, :] = tiles[t][k * 16 + 8 : k * 16 + 16]
+            for t in range(4):
+                to = (u * 4 + t) * 8
+                for k in range(4):
+                    kept_ref[k, to : to + 8, :] = tiles[t][k * 8 : k * 8 + 8]
+                    if k == 2:
+                        soon_ref[to : to + 8, :] = tiles[t][k * 8 + 32 : k * 8 + 40]
+                    else:
+                        later_ref[min(k, 2), to : to + 8, :] = tiles[t][k * 8 + 32 : k * 8 + 40]
 
 
 def kernel_c(kept_ref, got_ref, *refs):
     arrived, (gates_ref, factors_ref, out_ref) = refs[:3], refs[3:]
-    block_2 = (gates_ref[2, 0], gates_ref[2, 1])
-    block_4 = (gates_ref[3, 0], gates_ref[3, 1])
-    columns = []
-    for xl in range(4):
-        parts = []
-        for part in range(2):
-            rows = pl.ds(part * 4 + xl, 16, stride=8)
-            parts += [kept_ref[0, rows, :], got_ref[0, rows, :]]
-            for ref in (arrived[2], arrived[0], arrived[1]):
-                parts += [ref[0, rows, :], ref[1, rows, :]]
-        columns.append(jnp.concatenate(parts, axis=0))
-    result = product(mul, block_2, jnp.concatenate(columns, axis=1))
-    rotated = [
-        rotate(
-            (factors_ref[1, 0, xl], factors_ref[1, 1, xl]),
-            result[:128, xl * 128 : (xl + 1) * 128],
-            result[128:, xl * 128 : (xl + 1) * 128],
-        )
-        for xl in range(4)
-    ]
-    rows = []
-    for gb in range(8):
-        for xl in range(4):
-            real, imag = rotated[xl]
-            rows.append(
-                jnp.concatenate(
-                    [real[gb * 16 : (gb + 1) * 16], imag[gb * 16 : (gb + 1) * 16]], axis=1
+    rotated = []
+    for start in range(0, 4, 2):
+        columns = []
+        for xl in range(start, start + 2):
+            parts = []
+            for part in range(2):
+                rows = pl.ds(part * 4 + xl, 16, stride=8)
+                parts += [kept_ref[0, rows, :], got_ref[0, rows, :]]
+                for ref in (arrived[2], arrived[0], arrived[1]):
+                    parts += [ref[0, rows, :], ref[1, rows, :]]
+            columns.append(jnp.concatenate(parts, axis=0))
+        result = product(mul, gates_ref[2], jnp.concatenate(columns, axis=1))
+        for at in range(2):
+            rotated.append(
+                rotate(
+                    (factors_ref[1, 0, start + at], factors_ref[1, 1, start + at]),
+                    result[:128, at * 128 : (at + 1) * 128],
+                    result[128:, at * 128 : (at + 1) * 128],
                 )
             )
-    result = product(mul_t, block_4, jnp.concatenate(rows, axis=0))
-    for pair in range(4):
-        values = result[:, pair * 128 : (pair + 1) * 128]
-        tiles = swap_bit([values[:128], values[128:]], 0, 6)
-        for last in range(2):
-            gb = pair * 2 + last
-            for ah in range(4):
-                out_ref[pl.ds(gb * 4 + ah, 32, stride=32), :] = tiles[last][ah * 32 : (ah + 1) * 32]
+    for start in range(0, 4, 2):
+        rows = []
+        for gb in range(2 * start, 2 * (start + 2)):
+            for real, imag in rotated:
+                at = slice(gb * 16, (gb + 1) * 16)
+                rows.append(jnp.concatenate([real[at], imag[at]], axis=1))
+        result = product(mul_t, gates_ref[3], jnp.concatenate(rows, axis=0))
+        for pair in range(start, start + 2):
+            values = result[:, (pair - start) * 128 : (pair - start + 1) * 128]
+            tiles = swap_bit([values[:128], values[128:]], 0, 6)
+            for last in range(2):
+                start_row = (pair // 2) * 512 + (pair % 2 * 2 + last) * 4
+                for ah in range(4):
+                    rows = pl.ds(start_row + ah, 32, stride=16)
+                    out_ref[rows, :] = tiles[last][ah * 32 : (ah + 1) * 32]
 
 
 def kernel_d(amps_ref, gates_ref, out_hbm, out, sems):
-    block = (gates_ref[4, 0], gates_ref[4, 1])
     written = []
-    for b13 in range(2):
+    for half in range(2):
         rows = []
-        for b7 in range(2):
-            tiles = []
-            for xb in range(8):
-                start = b7 * 512 + xb * 64 + b13 * 8
-                tiles.append(
-                    jnp.concatenate(
-                        [amps_ref[start + 16 * at : start + 16 * at + 8, :] for at in range(4)], axis=0
-                    )
-                )
-            tiles = swap_bit(swap_bit(swap_bit(tiles, 2, 6), 1, 5), 0, 4)
-            for xl in range(4):
-                rows.append(jnp.concatenate([tiles[xl], tiles[4 + xl]], axis=1))
-        result = product(mul_t, block, jnp.concatenate(rows, axis=0), values_left=True)
-        for b7, xl, b11, b8, b12 in itertools.product(range(2), range(4), *[range(2)] * 3):
-            at = (b7 * 4 + xl) * 32 + b11 * 16 + b8 * 8 + b12 * 4
-            to = b13 * 64 + b12 * 32 + b11 * 16 + xl * 4 + b8 * 2 + b7
+        for ah in range(half * 2, half * 2 + 2):
+            for mid in range(4):
+                tiles = [
+                    amps_ref[pl.ds(xb * 128 + mid * 32 + ah, 8, stride=4), :] for xb in range(8)
+                ]
+                tiles = swap_bit(swap_bit(swap_bit(tiles, 2, 6), 1, 5), 0, 4)
+                for xl in range(4):
+                    rows.append(jnp.concatenate([tiles[xl], tiles[4 + xl]], axis=1))
+        result = product(mul_t, gates_ref[4], jnp.concatenate(rows, axis=0), values_left=True)
+        for at, (ah, mid, xl) in enumerate(itertools.product(range(2), range(4), range(4))):
+            to = (half * 2 + ah) * 128 + xl * 4 + mid
             for part in range(2):
-                out[pl.ds(2 * to + part, 4, stride=256), :] = result[
-                    at : at + 4, part * 128 : (part + 1) * 128
+                out[pl.ds(2 * to + part, 8, stride=32), :] = result[
+                    at * 8 : at * 8 + 8, part * 128 : (part + 1) * 128
                 ]
-        for ah in range(4):
-            piece = pl.ds(ah * 256 + b13 * 128, 128)
-            written.append(
-                pltpu.make_async_copy(out.at[piece], out_hbm.at[piece], sems.at[b13 * 4 + ah])
-            )
-            written[-1].start()
+        piece = pl.ds(half * 512, 512)
+        written.append(pltpu.make_async_copy(out.at[piece], out_hbm.at[piece], sems.at[half]))
+        written[-1].start()
     for copy in written:
         copy.wait()
 
@@ -361,7 +359,7 @@
 VMEM = pl.BlockSpec(memory_space=pltpu.VMEM)
 HBM = pl.BlockSpec(memory_space=pltpu.HBM)
 TABLES = (
-    jax.ShapeDtypeStruct((5, 2, 256, 256), BF16),
+    jax.ShapeDtypeStruct((5, 256, 768), BF16),
     jax.ShapeDtypeStruct((2, 2, 4, 128, LANES), F32),
 )
 
@@ -404,16 +402,25 @@
             pltpu.SemaphoreType.DMA((4,)),
         ),
     )
-    state = exchange(state, ["zh", "y", "zl", "c"]).reshape(1024, LANES)
+    state = exchange(state, ["y", "zh", "zl", "c"]).reshape(1024, LANES)
     gates, factors = call(kernel_tables, "tables", TABLES, *shared)
-    half = jax.ShapeDtypeStruct((4, 128, LANES), F32)
-    kept, sent = call(kernel_b, "second_gates", (half, half), state, gates, factors)
-    got = from_partner(sent, "c", 1)
+    kept, soon, later = call(
+        kernel_b,
+        "second_gates",
+        [jax.ShapeDtypeStruct(shape, F32) for shape in ((4, 128, 128), (128, 128), (3, 128, 128))],
+        state,
+        gates,
+        factors,
+    )
+    soon = from_partner(soon, "c", 1)
+    later = from_partner(later, "c", 1)
+    got = {1: later[1], 2: soon, 3: later[2]}
     arrived = {k: from_partner(jnp.stack([kept[k], got[k]]), "x", k) for k in (2, 3, 1)}
+    got = later
     state = call(
         kernel_c, "third_gates", shape, kept, got, arrived[2], arrived[3], arrived[1], gates, factors
     )
-    state = exchange(state, ["y", "zl", "c", "zh", "x"])
+    state = exchange(state, ["zh", "zl", "y", "c", "x"])
     state = call(
         kernel_d,
         "last_gate",
@@ -421,7 +428,7 @@
         state,
         gates,
         out_space=HBM,
-        scratch=(pltpu.VMEM((1024, LANES), F32), pltpu.SemaphoreType.DMA((8,))),
+        scratch=(pltpu.VMEM((1024, LANES), F32), pltpu.SemaphoreType.DMA((2,))),
     )
     return state.reshape(512, 2, LANES).transpose(1, 0, 2).reshape(2, 65536)
 

time: 78 us -> 77.6 us (level)
  waiting for transfers between devices: 22.3 us -> 19.9 us
  blocking collectives: 27.2 us -> 29.1 us
    all_to_all x1, blocking collectives: 27.2 us -> 29.1 us  [exchange(): lax.all_to_all(parts, AXES, 0, 0, axis_index_groups=groups, tiled=True)]
    all_to_all x1, waiting for transfers between devices: 15.4 us -> 13.9 us  [exchange(): lax.all_to_all(parts, AXES, 0, 0, axis_index_groups=groups, tiled=True)]
    ppermute x4 -> x5, waiting for transfers between devices: 6.96 us -> 6 us  [from_partner(): return lax.ppermute(value, AXES, pairs)]
    ppermute x4 -> x5, starting transfers between devices: 3.96 us -> 4.46 us  [from_partner(): return lax.ppermute(value, AXES, pairs)]
  transfers between devices with their start and end apart: 5 -> 6, of which waited for: 5 -> 5; matrix products, arithmetic and copies ran while one was open for 0% -> 0% of each run, Pallas kernels for 3% -> 3%
where the time goes in v3:
time: 77.6 us; the launch traced here: 77.3 us
  blocking collectives  29.1 us (38%)
  waiting for transfers between devices  19.9 us (26%)
  starting transfers between devices  17.6 us (23%)
  Pallas kernels  9.47 us (12%)
  local copies, waits for them, and re-layouts  1.16 us (1%)
    all_to_all x1, blocking collectives, exchange(): lax.all_to_all(parts, AXES, 0, 0, axis_index_groups=groups, tiled=True)  29.1 us
    all_to_all x1, waiting for transfers between devices, exchange(): lax.all_to_all(parts, AXES, 0, 0, axis_index_groups=groups, tiled=True)  13.9 us
    all_to_all x1, starting transfers between devices, exchange(): lax.all_to_all(parts, AXES, 0, 0, axis_index_groups=groups, tiled=True)  13.2 us
    pallas_call x5, Pallas kernels, call(): pl.pallas_call(kernel, out_shape=out_shape, in_specs=[space] * len(operan...  9.47 us
    ppermute x5, waiting for transfers between devices, from_partner(): return lax.ppermute(value, AXES, pairs)  6 us
    ppermute x5, starting transfers between devices, from_partner(): return lax.ppermute(value, AXES, pairs)  4.46 us
  transfers between devices with their start and end apart: 6, of which 5 were waited for; matrix products, arithmetic and copies ran while one was open for 0% of the time, Pallas kernels for 3%

profile of v3, /device:TPU:1, one launch (start us, length us, event | category | flops | bytes accessed | tf_op | source)
XLA Modules:
  0.0 77.3 jit_solution(3809184654154579358)
XLA Ops:
  0.0 0.0 copy-start.3
  0.0 3.0 %first_gate.1 = f32[64,16,128]{2,1,0:T(8,128)} custom-call(f32[1024,128]{1,0:T(8,128)} %bitcast.20, f32[6,2,128,128]{3,2,1,0:T(8,128)} %mats_ref.1, s32[6,7]{1,0:T(8,128)} %order_ref.1, s32[3,2,4]{2,1,0:T(2,128)} %bitcast.18, f32[3,4]{1,0:T(4,128)} %angles_ref.1), custom_call_target="tpu_custom_call" | custom-call | flops 400000000 | bytes 2000000 | tf_op jit(solution)/shard_map/first_gate/pallas_call | solution.py:368
  3.1 13.2 %all-to-all-start = ((f32[64,16,128]{2,1,0:T(8,128)}), f32[64,16,128]{2,1,0:T(8,128)S(1)}, u32[]{:S(2)}, u32[]{:S(2)}) async-start(f32[64,16,128]{2,1,0:T(8,128)} %first_gate.1), calls=%async_computation | async-start | bytes 1048576 | tf_op jit(solution)/shard_map/all_to_all | solution.py:32
  16.2 0.0 copy-done.3
  16.3 0.0 copy-done.1
  16.3 0.0 copy-done.2
  16.3 0.0 copy-start
  16.3 1.1 %copy-done = f32[6,2,128,128]{3,2,1,0:T(8,128)S(1)} copy-done((f32[6,2,128,128]{3,2,1,0:T(8,128)S(1)}, f32[6,2,128,128]{3,2,1,0:T(8,128)}, u32[]{:S(2)}) %copy-start) | copy-done | bytes 786456
  17.4 2.3 %tables.1 = (bf16[5,256,768]{2,1,0:T(8,128)(2,1)S(1)}, f32[2,2,4,128,128]{4,3,2,1,0:T(8,128)S(1)}) custom-call(f32[6,2,128,128]{3,2,1,0:T(8,128)S(1)} %copy-done, s32[6,7]{1,0:T(8,128)S(1)} %copy-done.1, s32[3,2,4]{2,1,0:T(2,128)S(1)} %bitcast.19, f32[3,4]{1,0:T(4,128)S(1)} %copy-done.3), custom_call_target="tpu_custom_call" | custom-call | flops 400000000 | bytes 2000000 | tf_op jit(solution)/shard_map/tables/pallas_call | solution.py:368
  19.7 13.9 %all-to-all-done = f32[64,16,128]{2,1,0:T(8,128)S(1)} async-done(((f32[64,16,128]{2,1,0:T(8,128)}), f32[64,16,128]{2,1,0:T(8,128)S(1)}, u32[]{:S(2)}, u32[]{:S(2)}) %all-to-all-start) | async-done | bytes 524320 | tf_op jit(solution)/shard_map/all_to_all | solution.py:32
  33.6 1.5 %second_gates.1 = (f32[4,128,128]{2,1,0:T(8,128)S(1)}, f32[128,128]{1,0:T(8,128)S(1)}, f32[3,128,128]{2,1,0:T(8,128)S(1)}) custom-call(f32[1024,128]{1,0:T(8,128)S(1)} %bitcast.15, bf16[5,256,768]{2,1,0:T(8,128)(2,1)S(1)} %get-tuple-element.10.gates_ref.refs_3_, f32[2,2,4,128,128]{4,3,2,1,0:T(8,128)S(1)} %get-tuple-element.11.factors_ref.refs_4_), custom_call_target="tpu_custom_call" | custom-call | flops 400000000 | bytes 2000000 | tf_op jit(solution)/shard_map/second_gates/pallas_call | solution.py:368
  35.1 0.4 collective-permute-start.1
  35.5 0.2 collective-permute-start
  35.7 0.7 collective-permute-done.1
  36.4 2.8 %collective-permute-start.2 = (f32[2,128,128]{2,1,0:T(8,128)S(1)}, f32[2,128,128]{2,1,0:T(8,128)S(1)}, u32[]{:S(2)}, u32[]{:S(2)}) collective-permute-start(f32[2,128,128]{2,1,0:T(8,128)S(1)} %pad_maximum_fusion), channel_id=1, source_target_pairs={{0,2},{1,3},{2,0},{3,1},{4,6},{5,7},{6,4},{7,5},{8,10},{9,11},{10,... | collective-permute-start | bytes 393224 | tf_op jit(solution)/shard_map/ppermute | solution.py:40
  39.3 0.0 collective-permute-done.got_ref
  39.3 0.9 %collective-permute-start.3 = (f32[2,128,128]{2,1,0:T(8,128)S(1)}, f32[2,128,128]{2,1,0:T(8,128)S(1)}, u32[]{:S(2)}, u32[]{:S(2)}) collective-permute-start(f32[2,128,128]{2,1,0:T(8,128)S(1)} %pad_maximum_fusion.1), channel_id=1, source_target_pairs={{0,3},{1,2},{2,1},{3,0},{4,7},{5,6},{6,5},{7,4},{8,11},{9,10},{10,... | collective-permute-start | bytes 393224 | tf_op jit(solution)/shard_map/ppermute | solution.py:40
  40.3 0.1 collective-permute-start.4
  40.4 2.4 %collective-permute-done.2.refs_0_ = f32[2,128,128]{2,1,0:T(8,128)S(1)} collective-permute-done((f32[2,128,128]{2,1,0:T(8,128)S(1)}, f32[2,128,128]{2,1,0:T(8,128)S(1)}, u32[]{:S(2)}, u32[]{:S(2)}) %collective-permute-start.2) | collective-permute-done | bytes 131104 | tf_op jit(solution)/shard_map/ppermute | solution.py:40
  42.8 2.7 %collective-permute-done.3.refs_1_ = f32[2,128,128]{2,1,0:T(8,128)S(1)} collective-permute-done((f32[2,128,128]{2,1,0:T(8,128)S(1)}, f32[2,128,128]{2,1,0:T(8,128)S(1)}, u32[]{:S(2)}, u32[]{:S(2)}) %collective-permute-start.3) | collective-permute-done | bytes 131104 | tf_op jit(solution)/shard_map/ppermute | solution.py:40
  45.5 0.1 collective-permute-done.4.refs_2_
  45.6 1.0 %third_gates.1 = f32[1024,128]{1,0:T(8,128)S(1)} custom-call(f32[4,128,128]{2,1,0:T(8,128)S(1)} %get-tuple-element.12.kept_ref, f32[3,128,128]{2,1,0:T(8,128)S(1)} %collective-permute-done.got_ref, f32[2,128,128]{2,1,0:T(8,128)S(1)} %collective-permute-done.2.refs_0_, f32[2,128,128]{2,1,0:T(8,128)S(1)} %collective-permute-done.3.refs_1_, ...), custom_call_target="tpu_custom_call" | custom-call | flops 400000000 | bytes 2000000 | tf_op jit(solution)/shard_map/third_gates/pallas_call | solution.py:368
  46.6 29.1 %all_to_all.10 = f32[256,4,128]{2,1,0:T(4,128)S(1)} all-to-all(f32[256,4,128]{2,1,0:T(4,128)S(1)} %bitcast.16), channel_id=1, replica_groups={{0,1,2,3,8,9,10,11,64,65,66,67,72,73,74,75,128,129,130,131,136,137,138,..., dimensions={0} | all-to-all | bytes 1048576 | tf_op jit(solution)/shard_map/all_to_all | solution.py:32
  75.7 1.6 %last_gate.1 = f32[1024,128]{1,0:T(8,128)} custom-call(f32[1024,128]{1,0:T(8,128)S(1)} %bitcast.17, bf16[5,256,768]{2,1,0:T(8,128)(2,1)S(1)} %get-tuple-element.10.gates_ref.refs_3_), custom_call_target="tpu_custom_call" | custom-call | flops 400000000 | bytes 2000000 | tf_op jit(solution)/shard_map/last_gate/pallas_call | solution.py:368
  (7 shorter events, 0.1 us)
Async XLA Ops:
  0.0 16.2 %copy-start.3 = (f32[3,4]{1,0:T(4,128)S(1)}, f32[3,4]{1,0:T(4,128)}, u32[]{:S(2)}) copy-start(f32[3,4]{1,0:T(4,128)} %angles_ref.1) | copy-start | bytes 148
  0.0 16.3 %copy-start.1 = (s32[6,7]{1,0:T(8,128)S(1)}, s32[6,7]{1,0:T(8,128)}, u32[]{:S(2)}) copy-start(s32[6,7]{1,0:T(8,128)} %order_ref.1) | copy-start | bytes 508
  0.0 16.3 %copy-start.2 = (s32[3,4,2]{1,2,0:T(2,128)S(1)}, s32[3,4,2]{1,2,0:T(2,128)}, u32[]{:S(2)}) copy-start(s32[3,4,2]{1,2,0:T(2,128)} %param.8) | copy-start | bytes 292
  3.1 30.5 %all-to-all-start = ((f32[64,16,128]{2,1,0:T(8,128)}), f32[64,16,128]{2,1,0:T(8,128)S(1)}, u32[]{:S(2)}, u32[]{:S(2)}) async-start(f32[64,16,128]{2,1,0:T(8,128)} %first_gate.1), calls=%async_computation | async-start | bytes 1048576 | tf_op jit(solution)/shard_map/all_to_all | solution.py:32
  16.3 1.1 %copy-start = (f32[6,2,128,128]{3,2,1,0:T(8,128)S(1)}, f32[6,2,128,128]{3,2,1,0:T(8,128)}, u32[]{:S(2)}) copy-start(f32[6,2,128,128]{3,2,1,0:T(8,128)} %mats_ref.1) | copy-start | bytes 2359300
  35.1 1.3 %collective-permute-start.1 = (f32[128,128]{1,0:T(8,128)S(1)}, f32[128,128]{1,0:T(8,128)S(1)}, u32[]{:S(2)}, u32[]{:S(2)}) collective-permute-start(f32[128,128]{1,0:T(8,128)S(1)} %get-tuple-element.14), channel_id=1, source_target_pairs={{0,8},{8,0},{1,9},{9,1},{2,10},{10,2},{3,11},{11,3},{4,12},{12,4},... | collective-permute-start | bytes 196616 | tf_op jit(solution)/shard_map/ppermute | solution.py:40
  35.5 3.8 %collective-permute-start = (f32[3,128,128]{2,1,0:T(8,128)S(1)}, f32[3,128,128]{2,1,0:T(8,128)S(1)}, u32[]{:S(2)}, u32[]{:S(2)}) collective-permute-start(f32[3,128,128]{2,1,0:T(8,128)S(1)} %get-tuple-element.13), channel_id=1, source_target_pairs={{0,8},{8,0},{1,9},{9,1},{2,10},{10,2},{3,11},{11,3},{4,12},{12,4},... | collective-permute-start | bytes 589832 | tf_op jit(solution)/shard_map/ppermute | solution.py:40
  36.4 6.4 %collective-permute-start.2 = (f32[2,128,128]{2,1,0:T(8,128)S(1)}, f32[2,128,128]{2,1,0:T(8,128)S(1)}, u32[]{:S(2)}, u32[]{:S(2)}) collective-permute-start(f32[2,128,128]{2,1,0:T(8,128)S(1)} %pad_maximum_fusion), channel_id=1, source_target_pairs={{0,2},{1,3},{2,0},{3,1},{4,6},{5,7},{6,4},{7,5},{8,10},{9,11},{10,... | collective-permute-start | bytes 393224 | tf_op jit(solution)/shard_map/ppermute | solution.py:40
  39.3 6.2 %collective-permute-start.3 = (f32[2,128,128]{2,1,0:T(8,128)S(1)}, f32[2,128,128]{2,1,0:T(8,128)S(1)}, u32[]{:S(2)}, u32[]{:S(2)}) collective-permute-start(f32[2,128,128]{2,1,0:T(8,128)S(1)} %pad_maximum_fusion.1), channel_id=1, source_target_pairs={{0,3},{1,2},{2,1},{3,0},{4,7},{5,6},{6,5},{7,4},{8,11},{9,10},{10,... | collective-permute-start | bytes 393224 | tf_op jit(solution)/shard_map/ppermute | solution.py:40
  40.3 5.4 %collective-permute-start.4 = (f32[2,128,128]{2,1,0:T(8,128)S(1)}, f32[2,128,128]{2,1,0:T(8,128)S(1)}, u32[]{:S(2)}, u32[]{:S(2)}) collective-permute-start(f32[2,128,128]{2,1,0:T(8,128)S(1)} %pad_maximum_fusion.2), channel_id=1, source_target_pairs={{0,1},{1,0},{2,3},{3,2},{4,5},{5,4},{6,7},{7,6},{8,9},{9,8},{10,11... | collective-permute-start | bytes 393224 | tf_op jit(solution)/shard_map/ppermute | solution.py:40

commit v4 on v3

--- a/solution.py
+++ b/solution.py
@@ -222,9 +222,9 @@
             factors_ref[0, part, u] = factor[part]
     index = (row // 16) * (1 << 16) + (row % 16) + (lane // 32) * (1 << 14) + (lane % 32) * (1 << 19)
     phase = Phase(pairs_ref, angles_ref, 2, index)
-    device = held + core * (1 << 13) + x * (1 << 11)
+    device = held + core * (1 << 11) + x * (1 << 9)
     for xl in range(4):
-        factor = phase.factor(device + xl * 512)
+        factor = phase.factor(device + xl * (1 << 12))
         for part in range(2):
             factors_ref[1, part, xl] = factor[part]
     natural = iota(0)
@@ -233,7 +233,7 @@
     for slot, gate in enumerate((0, 3, 2, 4, 5)):
         rows = columns = natural
         if gate == 3:
-            rows = natural ^ (core * 16 + x * 4)
+            rows = take_bits(natural, (3, 4, 0, 1, 2, 5, 6)) ^ (core * 4 + x)
         if gate == 2:
             columns = arrived ^ (x * 16 + core * 8)
         if gate == 4:
@@ -344,9 +344,9 @@
                     rows.append(jnp.concatenate([tiles[xl], tiles[4 + xl]], axis=1))
         result = product(mul_t, gates_ref[4], jnp.concatenate(rows, axis=0), values_left=True)
         for at, (ah, mid, xl) in enumerate(itertools.product(range(2), range(4), range(4))):
-            to = (half * 2 + ah) * 128 + xl * 4 + mid
+            to = (half * 2 + ah) * 128 + xl * 32 + mid
             for part in range(2):
-                out[pl.ds(2 * to + part, 8, stride=32), :] = result[
+                out[pl.ds(2 * to + part, 8, stride=8), :] = result[
                     at * 8 : at * 8 + 8, part * 128 : (part + 1) * 128
                 ]
         piece = pl.ds(half * 512, 512)

time: 77.6 us -> 77.4 us (level)
  no operation moved by 1% of the time
where the time goes in v4:
time: 77.4 us; the launch traced here: 77.2 us
  blocking collectives  29.1 us (38%)
  waiting for transfers between devices  19.9 us (26%)
  starting transfers between devices  17.6 us (23%)
  Pallas kernels  9.32 us (12%)
  local copies, waits for them, and re-layouts  1.16 us (1%)
    all_to_all x1, blocking collectives, exchange(): lax.all_to_all(parts, AXES, 0, 0, axis_index_groups=groups, tiled=True)  29.1 us
    all_to_all x1, waiting for transfers between devices, exchange(): lax.all_to_all(parts, AXES, 0, 0, axis_index_groups=groups, tiled=True)  13.9 us
    all_to_all x1, starting transfers between devices, exchange(): lax.all_to_all(parts, AXES, 0, 0, axis_index_groups=groups, tiled=True)  13.2 us
    pallas_call x5, Pallas kernels, call(): pl.pallas_call(kernel, out_shape=out_shape, in_specs=[space] * len(operan...  9.32 us
    ppermute x5, waiting for transfers between devices, from_partner(): return lax.ppermute(value, AXES, pairs)  6 us
    ppermute x5, starting transfers between devices, from_partner(): return lax.ppermute(value, AXES, pairs)  4.46 us
  transfers between devices with their start and end apart: 6, of which 5 were waited for; matrix products, arithmetic and copies ran while one was open for 0% of the time, Pallas kernels for 3%

profile of v4, /device:TPU:1, one launch (start us, length us, event | category | flops | bytes accessed | tf_op | source)
XLA Modules:
  0.0 77.2 jit_solution(2278257391891184044)
XLA Ops:
  0.0 0.0 copy-start.3
  0.0 3.0 %first_gate.1 = f32[64,16,128]{2,1,0:T(8,128)} custom-call(f32[1024,128]{1,0:T(8,128)} %bitcast.20, f32[6,2,128,128]{3,2,1,0:T(8,128)} %mats_ref.1, s32[6,7]{1,0:T(8,128)} %order_ref.1, s32[3,2,4]{2,1,0:T(2,128)} %bitcast.18, f32[3,4]{1,0:T(4,128)} %angles_ref.1), custom_call_target="tpu_custom_call" | custom-call | flops 400000000 | bytes 2000000 | tf_op jit(solution)/shard_map/first_gate/pallas_call | solution.py:368
  3.1 13.2 %all-to-all-start = ((f32[64,16,128]{2,1,0:T(8,128)}), f32[64,16,128]{2,1,0:T(8,128)S(1)}, u32[]{:S(2)}, u32[]{:S(2)}) async-start(f32[64,16,128]{2,1,0:T(8,128)} %first_gate.1), calls=%async_computation | async-start | bytes 1048576 | tf_op jit(solution)/shard_map/all_to_all | solution.py:32
  16.2 0.0 copy-done.3
  16.3 0.0 copy-done.1
  16.3 0.0 copy-done.2
  16.3 0.0 copy-start
  16.3 1.1 %copy-done = f32[6,2,128,128]{3,2,1,0:T(8,128)S(1)} copy-done((f32[6,2,128,128]{3,2,1,0:T(8,128)S(1)}, f32[6,2,128,128]{3,2,1,0:T(8,128)}, u32[]{:S(2)}) %copy-start) | copy-done | bytes 786456
  17.4 2.3 %tables.1 = (bf16[5,256,768]{2,1,0:T(8,128)(2,1)S(1)}, f32[2,2,4,128,128]{4,3,2,1,0:T(8,128)S(1)}) custom-call(f32[6,2,128,128]{3,2,1,0:T(8,128)S(1)} %copy-done, s32[6,7]{1,0:T(8,128)S(1)} %copy-done.1, s32[3,2,4]{2,1,0:T(2,128)S(1)} %bitcast.19, f32[3,4]{1,0:T(4,128)S(1)} %copy-done.3), custom_call_target="tpu_custom_call" | custom-call | flops 400000000 | bytes 2000000 | tf_op jit(solution)/shard_map/tables/pallas_call | solution.py:368
  19.7 13.9 %all-to-all-done = f32[64,16,128]{2,1,0:T(8,128)S(1)} async-done(((f32[64,16,128]{2,1,0:T(8,128)}), f32[64,16,128]{2,1,0:T(8,128)S(1)}, u32[]{:S(2)}, u32[]{:S(2)}) %all-to-all-start) | async-done | bytes 524320 | tf_op jit(solution)/shard_map/all_to_all | solution.py:32
  33.6 1.5 %second_gates.1 = (f32[4,128,128]{2,1,0:T(8,128)S(1)}, f32[128,128]{1,0:T(8,128)S(1)}, f32[3,128,128]{2,1,0:T(8,128)S(1)}) custom-call(f32[1024,128]{1,0:T(8,128)S(1)} %bitcast.15, bf16[5,256,768]{2,1,0:T(8,128)(2,1)S(1)} %get-tuple-element.10.gates_ref.refs_3_, f32[2,2,4,128,128]{4,3,2,1,0:T(8,128)S(1)} %get-tuple-element.11.factors_ref.refs_4_), custom_call_target="tpu_custom_call" | custom-call | flops 400000000 | bytes 2000000 | tf_op jit(solution)/shard_map/second_gates/pallas_call | solution.py:368
  35.1 0.4 collective-permute-start.1
  35.5 0.2 collective-permute-start
  35.7 0.7 collective-permute-done.1
  36.4 2.8 %collective-permute-start.2 = (f32[2,128,128]{2,1,0:T(8,128)S(1)}, f32[2,128,128]{2,1,0:T(8,128)S(1)}, u32[]{:S(2)}, u32[]{:S(2)}) collective-permute-start(f32[2,128,128]{2,1,0:T(8,128)S(1)} %pad_maximum_fusion), channel_id=1, source_target_pairs={{0,2},{1,3},{2,0},{3,1},{4,6},{5,7},{6,4},{7,5},{8,10},{9,11},{10,... | collective-permute-start | bytes 393224 | tf_op jit(solution)/shard_map/ppermute | solution.py:40
  39.3 0.0 collective-permute-done.got_ref
  39.3 0.9 %collective-permute-start.3 = (f32[2,128,128]{2,1,0:T(8,128)S(1)}, f32[2,128,128]{2,1,0:T(8,128)S(1)}, u32[]{:S(2)}, u32[]{:S(2)}) collective-permute-start(f32[2,128,128]{2,1,0:T(8,128)S(1)} %pad_maximum_fusion.1), channel_id=1, source_target_pairs={{0,3},{1,2},{2,1},{3,0},{4,7},{5,6},{6,5},{7,4},{8,11},{9,10},{10,... | collective-permute-start | bytes 393224 | tf_op jit(solution)/shard_map/ppermute | solution.py:40
  40.3 0.1 collective-permute-start.4
  40.4 2.4 %collective-permute-done.2.refs_0_ = f32[2,128,128]{2,1,0:T(8,128)S(1)} collective-permute-done((f32[2,128,128]{2,1,0:T(8,128)S(1)}, f32[2,128,128]{2,1,0:T(8,128)S(1)}, u32[]{:S(2)}, u32[]{:S(2)}) %collective-permute-start.2) | collective-permute-done | bytes 131104 | tf_op jit(solution)/shard_map/ppermute | solution.py:40
  42.8 2.7 %collective-permute-done.3.refs_1_ = f32[2,128,128]{2,1,0:T(8,128)S(1)} collective-permute-done((f32[2,128,128]{2,1,0:T(8,128)S(1)}, f32[2,128,128]{2,1,0:T(8,128)S(1)}, u32[]{:S(2)}, u32[]{:S(2)}) %collective-permute-start.3) | collective-permute-done | bytes 131104 | tf_op jit(solution)/shard_map/ppermute | solution.py:40
  45.5 0.1 collective-permute-done.4.refs_2_
  45.6 1.0 %third_gates.1 = f32[1024,128]{1,0:T(8,128)S(1)} custom-call(f32[4,128,128]{2,1,0:T(8,128)S(1)} %get-tuple-element.12.kept_ref, f32[3,128,128]{2,1,0:T(8,128)S(1)} %collective-permute-done.got_ref, f32[2,128,128]{2,1,0:T(8,128)S(1)} %collective-permute-done.2.refs_0_, f32[2,128,128]{2,1,0:T(8,128)S(1)} %collective-permute-done.3.refs_1_, ...), custom_call_target="tpu_custom_call" | custom-call | flops 400000000 | bytes 2000000 | tf_op jit(solution)/shard_map/third_gates/pallas_call | solution.py:368
  46.6 29.1 %all_to_all.10 = f32[256,4,128]{2,1,0:T(4,128)S(1)} all-to-all(f32[256,4,128]{2,1,0:T(4,128)S(1)} %bitcast.16), channel_id=1, replica_groups={{0,1,2,3,8,9,10,11,64,65,66,67,72,73,74,75,128,129,130,131,136,137,138,..., dimensions={0} | all-to-all | bytes 1048576 | tf_op jit(solution)/shard_map/all_to_all | solution.py:32
  75.7 1.5 %last_gate.1 = f32[1024,128]{1,0:T(8,128)} custom-call(f32[1024,128]{1,0:T(8,128)S(1)} %bitcast.17, bf16[5,256,768]{2,1,0:T(8,128)(2,1)S(1)} %get-tuple-element.10.gates_ref.refs_3_), custom_call_target="tpu_custom_call" | custom-call | flops 400000000 | bytes 2000000 | tf_op jit(solution)/shard_map/last_gate/pallas_call | solution.py:368
  (7 shorter events, 0.1 us)
Async XLA Ops:
  0.0 16.2 %copy-start.3 = (f32[3,4]{1,0:T(4,128)S(1)}, f32[3,4]{1,0:T(4,128)}, u32[]{:S(2)}) copy-start(f32[3,4]{1,0:T(4,128)} %angles_ref.1) | copy-start | bytes 148
  0.0 16.3 %copy-start.1 = (s32[6,7]{1,0:T(8,128)S(1)}, s32[6,7]{1,0:T(8,128)}, u32[]{:S(2)}) copy-start(s32[6,7]{1,0:T(8,128)} %order_ref.1) | copy-start | bytes 508
  0.0 16.3 %copy-start.2 = (s32[3,4,2]{1,2,0:T(2,128)S(1)}, s32[3,4,2]{1,2,0:T(2,128)}, u32[]{:S(2)}) copy-start(s32[3,4,2]{1,2,0:T(2,128)} %param.8) | copy-start | bytes 292
  3.1 30.5 %all-to-all-start = ((f32[64,16,128]{2,1,0:T(8,128)}), f32[64,16,128]{2,1,0:T(8,128)S(1)}, u32[]{:S(2)}, u32[]{:S(2)}) async-start(f32[64,16,128]{2,1,0:T(8,128)} %first_gate.1), calls=%async_computation | async-start | bytes 1048576 | tf_op jit(solution)/shard_map/all_to_all | solution.py:32
  16.3 1.1 %copy-start = (f32[6,2,128,128]{3,2,1,0:T(8,128)S(1)}, f32[6,2,128,128]{3,2,1,0:T(8,128)}, u32[]{:S(2)}) copy-start(f32[6,2,128,128]{3,2,1,0:T(8,128)} %mats_ref.1) | copy-start | bytes 2359300
  35.1 1.3 %collective-permute-start.1 = (f32[128,128]{1,0:T(8,128)S(1)}, f32[128,128]{1,0:T(8,128)S(1)}, u32[]{:S(2)}, u32[]{:S(2)}) collective-permute-start(f32[128,128]{1,0:T(8,128)S(1)} %get-tuple-element.14), channel_id=1, source_target_pairs={{0,8},{8,0},{1,9},{9,1},{2,10},{10,2},{3,11},{11,3},{4,12},{12,4},... | collective-permute-start | bytes 196616 | tf_op jit(solution)/shard_map/ppermute | solution.py:40
  35.5 3.8 %collective-permute-start = (f32[3,128,128]{2,1,0:T(8,128)S(1)}, f32[3,128,128]{2,1,0:T(8,128)S(1)}, u32[]{:S(2)}, u32[]{:S(2)}) collective-permute-start(f32[3,128,128]{2,1,0:T(8,128)S(1)} %get-tuple-element.13), channel_id=1, source_target_pairs={{0,8},{8,0},{1,9},{9,1},{2,10},{10,2},{3,11},{11,3},{4,12},{12,4},... | collective-permute-start | bytes 589832 | tf_op jit(solution)/shard_map/ppermute | solution.py:40
  36.4 6.4 %collective-permute-start.2 = (f32[2,128,128]{2,1,0:T(8,128)S(1)}, f32[2,128,128]{2,1,0:T(8,128)S(1)}, u32[]{:S(2)}, u32[]{:S(2)}) collective-permute-start(f32[2,128,128]{2,1,0:T(8,128)S(1)} %pad_maximum_fusion), channel_id=1, source_target_pairs={{0,2},{1,3},{2,0},{3,1},{4,6},{5,7},{6,4},{7,5},{8,10},{9,11},{10,... | collective-permute-start | bytes 393224 | tf_op jit(solution)/shard_map/ppermute | solution.py:40
  39.3 6.2 %collective-permute-start.3 = (f32[2,128,128]{2,1,0:T(8,128)S(1)}, f32[2,128,128]{2,1,0:T(8,128)S(1)}, u32[]{:S(2)}, u32[]{:S(2)}) collective-permute-start(f32[2,128,128]{2,1,0:T(8,128)S(1)} %pad_maximum_fusion.1), channel_id=1, source_target_pairs={{0,3},{1,2},{2,1},{3,0},{4,7},{5,6},{6,5},{7,4},{8,11},{9,10},{10,... | collective-permute-start | bytes 393224 | tf_op jit(solution)/shard_map/ppermute | solution.py:40
  40.3 5.4 %collective-permute-start.4 = (f32[2,128,128]{2,1,0:T(8,128)S(1)}, f32[2,128,128]{2,1,0:T(8,128)S(1)}, u32[]{:S(2)}, u32[]{:S(2)}) collective-permute-start(f32[2,128,128]{2,1,0:T(8,128)S(1)} %pad_maximum_fusion.2), channel_id=1, source_target_pairs={{0,1},{1,0},{2,3},{3,2},{4,5},{5,4},{6,7},{7,6},{8,9},{9,8},{10,11... | collective-permute-start | bytes 393224 | tf_op jit(solution)/shard_map/ppermute | solution.py:40

commit v5 on v4

--- a/solution.py
+++ b/solution.py
@@ -228,7 +228,7 @@
         for part in range(2):
             factors_ref[1, part, xl] = factor[part]
     natural = iota(0)
-    arrived = take_bits(natural, (0, 1, 2, 6, 3, 4, 5))
+    arrived = take_bits(natural, (0, 1, 2, 6, 3, 5, 4))
     leaving = take_bits(natural, (0, 3, 4, 1, 2, 5, 6))
     for slot, gate in enumerate((0, 3, 2, 4, 5)):
         rows = columns = natural
@@ -241,7 +241,13 @@
         blocks = gate_block(
             mats_ref.at[gate], order_ref, gate, rows, None if rows is columns else columns
         )
-        block = thrice(*full_block(blocks))
+        full = full_block(blocks)
+        block = thrice(*full)
+        if gate == 2:
+            full = [half.astype(F32) for half in full]
+            early = [jnp.concatenate([half[:, :64], half[:, 128:192]], axis=1) for half in full]
+            late = [jnp.concatenate([half[:, 64:128], half[:, 192:]], axis=1) for half in full]
+            block = jnp.concatenate([thrice(*early), thrice(*late)], axis=1).astype(BF16)
         if gate == 3:
             block = block.astype(F32).reshape(2, 32, 4, 768)
             block = jnp.concatenate([block[0], block[1]], axis=1).reshape(256, 768).astype(BF16)
@@ -291,20 +297,31 @@
                         later_ref[min(k, 2), to : to + 8, :] = tiles[t][k * 8 + 32 : k * 8 + 40]
 
 
-def kernel_c(kept_ref, got_ref, *refs):
-    arrived, (gates_ref, factors_ref, out_ref) = refs[:3], refs[3:]
+def some_rows(refs, xl):
+    parts = []
+    for part in range(2):
+        rows = pl.ds(part * 4 + xl, 16, stride=8)
+        for ref, at in refs:
+            parts.append(ref[at, rows, :])
+    return jnp.concatenate(parts, axis=0)
+
+
+def kernel_c1(kept_ref, got_ref, second_ref, gates_ref, out_ref):
+    refs = ((kept_ref, 0), (got_ref, 0), (second_ref, 0), (second_ref, 1))
+    for start in range(0, 4, 2):
+        columns = [some_rows(refs, xl) for xl in range(start, start + 2)]
+        lanes = slice(start * 128, (start + 2) * 128)
+        out_ref[:, lanes] = product(mul, gates_ref[2, :, :384], jnp.concatenate(columns, axis=1))
+
+
+def kernel_c(sum_ref, third_ref, first_ref, gates_ref, factors_ref, out_ref):
+    refs = ((first_ref, 0), (first_ref, 1), (third_ref, 0), (third_ref, 1))
     rotated = []
     for start in range(0, 4, 2):
-        columns = []
-        for xl in range(start, start + 2):
-            parts = []
-            for part in range(2):
-                rows = pl.ds(part * 4 + xl, 16, stride=8)
-                parts += [kept_ref[0, rows, :], got_ref[0, rows, :]]
-                for ref in (arrived[2], arrived[0], arrived[1]):
-                    parts += [ref[0, rows, :], ref[1, rows, :]]
-            columns.append(jnp.concatenate(parts, axis=0))
-        result = product(mul, gates_ref[2], jnp.concatenate(columns, axis=1))
+        columns = [some_rows(refs, xl) for xl in range(start, start + 2)]
+        lanes = slice(start * 128, (start + 2) * 128)
+        result = product(mul, gates_ref[2, :, 384:], jnp.concatenate(columns, axis=1))
+        result = result + sum_ref[:, lanes]
         for at in range(2):
             rotated.append(
                 rotate(
@@ -417,9 +434,16 @@
     got = {1: later[1], 2: soon, 3: later[2]}
     arrived = {k: from_partner(jnp.stack([kept[k], got[k]]), "x", k) for k in (2, 3, 1)}
     got = later
-    state = call(
-        kernel_c, "third_gates", shape, kept, got, arrived[2], arrived[3], arrived[1], gates, factors
+    total = call(
+        kernel_c1,
+        "third_gates_early",
+        jax.ShapeDtypeStruct((256, 512), F32),
+        kept,
+        got,
+        arrived[2],
+        gates,
     )
+    state = call(kernel_c, "third_gates", shape, total, arrived[3], arrived[1], gates, factors)
     state = exchange(state, ["zh", "zl", "y", "c", "x"])
     state = call(
         kernel_d,

time: 77.4 us -> 77.4 us (level)
    pallas_call x5 -> x6, Pallas kernels: 9.32 us -> 9.59 us  [call(): pl.pallas_call(kernel, out_shape=out_shape, in_specs=[space] * len(operan...]
where the time goes in v5:
time: 77.4 us; the launch traced here: 77.1 us
  blocking collectives  29.1 us (38%)
  waiting for transfers between devices  19.5 us (25%)
  starting transfers between devices  17.6 us (23%)
  Pallas kernels  9.59 us (12%)
  local copies, waits for them, and re-layouts  1.16 us (1%)
    all_to_all x1, blocking collectives, exchange(): lax.all_to_all(parts, AXES, 0, 0, axis_index_groups=groups, tiled=True)  29.1 us
    all_to_all x1, waiting for transfers between devices, exchange(): lax.all_to_all(parts, AXES, 0, 0, axis_index_groups=groups, tiled=True)  13.8 us
    all_to_all x1, starting transfers between devices, exchange(): lax.all_to_all(parts, AXES, 0, 0, axis_index_groups=groups, tiled=True)  13.2 us
    pallas_call x6, Pallas kernels, call(): pl.pallas_call(kernel, out_shape=out_shape, in_specs=[space] * len(operan...  9.59 us
    ppermute x5, waiting for transfers between devices, from_partner(): return lax.ppermute(value, AXES, pairs)  5.66 us
    ppermute x5, starting transfers between devices, from_partner(): return lax.ppermute(value, AXES, pairs)  4.46 us
  transfers between devices with their start and end apart: 6, of which 5 were waited for; matrix products, arithmetic and copies ran while one was open for 0% of the time, Pallas kernels for 3%

profile of v5, /device:TPU:1, one launch (start us, length us, event | category | flops | bytes accessed | tf_op | source)
XLA Modules:
  0.0 77.1 jit_solution(17042543917657147994)
XLA Ops:
  0.0 3.0 %first_gate.1 = f32[64,16,128]{2,1,0:T(8,128)} custom-call(f32[1024,128]{1,0:T(8,128)} %bitcast.20, f32[6,2,128,128]{3,2,1,0:T(8,128)} %mats_ref.1, s32[6,7]{1,0:T(8,128)} %order_ref.1, s32[3,2,4]{2,1,0:T(2,128)} %bitcast.18, f32[3,4]{1,0:T(4,128)} %angles_ref.1), custom_call_target="tpu_custom_call" | custom-call | flops 400000000 | bytes 2000000 | tf_op jit(solution)/shard_map/first_gate/pallas_call | solution.py:385
  3.1 13.2 %all-to-all-start = ((f32[64,16,128]{2,1,0:T(8,128)}), f32[64,16,128]{2,1,0:T(8,128)S(1)}, u32[]{:S(2)}, u32[]{:S(2)}) async-start(f32[64,16,128]{2,1,0:T(8,128)} %first_gate.1), calls=%async_computation | async-start | bytes 1048576 | tf_op jit(solution)/shard_map/all_to_all | solution.py:32
  16.2 0.0 copy-done.3
  16.3 0.0 copy-done.1
  16.3 0.0 copy-done.2
  16.3 0.0 copy-start
  16.3 1.1 %copy-done = f32[6,2,128,128]{3,2,1,0:T(8,128)S(1)} copy-done((f32[6,2,128,128]{3,2,1,0:T(8,128)S(1)}, f32[6,2,128,128]{3,2,1,0:T(8,128)}, u32[]{:S(2)}) %copy-start) | copy-done | bytes 786456
  17.4 2.3 %tables.1 = (bf16[5,256,768]{2,1,0:T(8,128)(2,1)S(1)}, f32[2,2,4,128,128]{4,3,2,1,0:T(8,128)S(1)}) custom-call(f32[6,2,128,128]{3,2,1,0:T(8,128)S(1)} %copy-done, s32[6,7]{1,0:T(8,128)S(1)} %copy-done.1, s32[3,2,4]{2,1,0:T(2,128)S(1)} %bitcast.19, f32[3,4]{1,0:T(4,128)S(1)} %copy-done.3), custom_call_target="tpu_custom_call" | custom-call | flops 400000000 | bytes 2000000 | tf_op jit(solution)/shard_map/tables/pallas_call | solution.py:385
  19.7 13.8 %all-to-all-done = f32[64,16,128]{2,1,0:T(8,128)S(1)} async-done(((f32[64,16,128]{2,1,0:T(8,128)}), f32[64,16,128]{2,1,0:T(8,128)S(1)}, u32[]{:S(2)}, u32[]{:S(2)}) %all-to-all-start) | async-done | bytes 524320 | tf_op jit(solution)/shard_map/all_to_all | solution.py:32
  33.6 1.5 %second_gates.1 = (f32[4,128,128]{2,1,0:T(8,128)S(1)}, f32[128,128]{1,0:T(8,128)S(1)}, f32[3,128,128]{2,1,0:T(8,128)S(1)}) custom-call(f32[1024,128]{1,0:T(8,128)S(1)} %bitcast.15, bf16[5,256,768]{2,1,0:T(8,128)(2,1)S(1)} %get-tuple-element.10.gates_ref, f32[2,2,4,128,128]{4,3,2,1,0:T(8,128)S(1)} %get-tuple-element.11.factors_ref), custom_call_target="tpu_custom_call" | custom-call | flops 400000000 | bytes 2000000 | tf_op jit(solution)/shard_map/second_gates/pallas_call | solution.py:385
  35.1 0.4 collective-permute-start.1
  35.5 0.2 collective-permute-start
  35.7 0.7 collective-permute-done.1
  36.4 2.8 %collective-permute-start.2 = (f32[2,128,128]{2,1,0:T(8,128)S(1)}, f32[2,128,128]{2,1,0:T(8,128)S(1)}, u32[]{:S(2)}, u32[]{:S(2)}) collective-permute-start(f32[2,128,128]{2,1,0:T(8,128)S(1)} %pad_maximum_fusion), channel_id=1, source_target_pairs={{0,2},{1,3},{2,0},{3,1},{4,6},{5,7},{6,4},{7,5},{8,10},{9,11},{10,... | collective-permute-start | bytes 393224 | tf_op jit(solution)/shard_map/ppermute | solution.py:40
  39.3 0.0 collective-permute-done.got_ref
  39.3 0.9 %collective-permute-start.3 = (f32[2,128,128]{2,1,0:T(8,128)S(1)}, f32[2,128,128]{2,1,0:T(8,128)S(1)}, u32[]{:S(2)}, u32[]{:S(2)}) collective-permute-start(f32[2,128,128]{2,1,0:T(8,128)S(1)} %pad_maximum_fusion.1), channel_id=1, source_target_pairs={{0,3},{1,2},{2,1},{3,0},{4,7},{5,6},{6,5},{7,4},{8,11},{9,10},{10,... | collective-permute-start | bytes 393224 | tf_op jit(solution)/shard_map/ppermute | solution.py:40
  40.3 0.1 collective-permute-start.4
  40.4 2.4 %collective-permute-done.2.second_ref = f32[2,128,128]{2,1,0:T(8,128)S(1)} collective-permute-done((f32[2,128,128]{2,1,0:T(8,128)S(1)}, f32[2,128,128]{2,1,0:T(8,128)S(1)}, u32[]{:S(2)}, u32[]{:S(2)}) %collective-permute-start.2) | collective-permute-done | bytes 131104 | tf_op jit(solution)/shard_map/ppermute | solution.py:40
  42.8 0.3 third_gates_early.1.sum_ref
  43.1 2.4 %collective-permute-done.3.third_ref = f32[2,128,128]{2,1,0:T(8,128)S(1)} collective-permute-done((f32[2,128,128]{2,1,0:T(8,128)S(1)}, f32[2,128,128]{2,1,0:T(8,128)S(1)}, u32[]{:S(2)}, u32[]{:S(2)}) %collective-permute-start.3) | collective-permute-done | bytes 131104 | tf_op jit(solution)/shard_map/ppermute | solution.py:40
  45.5 0.1 collective-permute-done.4.first_ref
  45.6 0.9 %third_gates.1 = f32[1024,128]{1,0:T(8,128)S(1)} custom-call(f32[256,512]{1,0:T(8,128)S(1)} %third_gates_early.1.sum_ref, f32[2,128,128]{2,1,0:T(8,128)S(1)} %collective-permute-done.3.third_ref, f32[2,128,128]{2,1,0:T(8,128)S(1)} %collective-permute-done.4.first_ref, bf16[5,256,768]{2,1,0:T(8,128)(2,1)S(1)} %get-tuple-element.10.gates_ref, ...), custom_call_target="tpu_custom_call" | custom-call | flops 400000000 | bytes 2000000 | tf_op jit(solution)/shard_map/third_gates/pallas_call | solution.py:385
  46.6 29.1 %all_to_all.10 = f32[256,4,128]{2,1,0:T(4,128)S(1)} all-to-all(f32[256,4,128]{2,1,0:T(4,128)S(1)} %bitcast.16), channel_id=1, replica_groups={{0,1,2,3,8,9,10,11,64,65,66,67,72,73,74,75,128,129,130,131,136,137,138,..., dimensions={0} | all-to-all | bytes 1048576 | tf_op jit(solution)/shard_map/all_to_all | solution.py:32
  75.6 1.5 %last_gate.1 = f32[1024,128]{1,0:T(8,128)} custom-call(f32[1024,128]{1,0:T(8,128)S(1)} %bitcast.17, bf16[5,256,768]{2,1,0:T(8,128)(2,1)S(1)} %get-tuple-element.10.gates_ref), custom_call_target="tpu_custom_call" | custom-call | flops 400000000 | bytes 2000000 | tf_op jit(solution)/shard_map/last_gate/pallas_call | solution.py:385
  (8 shorter events, 0.1 us)
Async XLA Ops:
  0.0 16.2 %copy-start.3 = (f32[3,4]{1,0:T(4,128)S(1)}, f32[3,4]{1,0:T(4,128)}, u32[]{:S(2)}) copy-start(f32[3,4]{1,0:T(4,128)} %angles_ref.1) | copy-start | bytes 148
  0.0 16.3 %copy-start.1 = (s32[6,7]{1,0:T(8,128)S(1)}, s32[6,7]{1,0:T(8,128)}, u32[]{:S(2)}) copy-start(s32[6,7]{1,0:T(8,128)} %order_ref.1) | copy-start | bytes 508
  0.0 16.3 %copy-start.2 = (s32[3,4,2]{1,2,0:T(2,128)S(1)}, s32[3,4,2]{1,2,0:T(2,128)}, u32[]{:S(2)}) copy-start(s32[3,4,2]{1,2,0:T(2,128)} %param.8) | copy-start | bytes 292
  3.1 30.5 %all-to-all-start = ((f32[64,16,128]{2,1,0:T(8,128)}), f32[64,16,128]{2,1,0:T(8,128)S(1)}, u32[]{:S(2)}, u32[]{:S(2)}) async-start(f32[64,16,128]{2,1,0:T(8,128)} %first_gate.1), calls=%async_computation | async-start | bytes 1048576 | tf_op jit(solution)/shard_map/all_to_all | solution.py:32
  16.3 1.1 %copy-start = (f32[6,2,128,128]{3,2,1,0:T(8,128)S(1)}, f32[6,2,128,128]{3,2,1,0:T(8,128)}, u32[]{:S(2)}) copy-start(f32[6,2,128,128]{3,2,1,0:T(8,128)} %mats_ref.1) | copy-start | bytes 2359300
  35.1 1.3 %collective-permute-start.1 = (f32[128,128]{1,0:T(8,128)S(1)}, f32[128,128]{1,0:T(8,128)S(1)}, u32[]{:S(2)}, u32[]{:S(2)}) collective-permute-start(f32[128,128]{1,0:T(8,128)S(1)} %get-tuple-element.14), channel_id=1, source_target_pairs={{0,8},{8,0},{1,9},{9,1},{2,10},{10,2},{3,11},{11,3},{4,12},{12,4},... | collective-permute-start | bytes 196616 | tf_op jit(solution)/shard_map/ppermute | solution.py:40
  35.5 3.8 %collective-permute-start = (f32[3,128,128]{2,1,0:T(8,128)S(1)}, f32[3,128,128]{2,1,0:T(8,128)S(1)}, u32[]{:S(2)}, u32[]{:S(2)}) collective-permute-start(f32[3,128,128]{2,1,0:T(8,128)S(1)} %get-tuple-element.13), channel_id=1, source_target_pairs={{0,8},{8,0},{1,9},{9,1},{2,10},{10,2},{3,11},{11,3},{4,12},{12,4},... | collective-permute-start | bytes 589832 | tf_op jit(solution)/shard_map/ppermute | solution.py:40
  36.4 6.4 %collective-permute-start.2 = (f32[2,128,128]{2,1,0:T(8,128)S(1)}, f32[2,128,128]{2,1,0:T(8,128)S(1)}, u32[]{:S(2)}, u32[]{:S(2)}) collective-permute-start(f32[2,128,128]{2,1,0:T(8,128)S(1)} %pad_maximum_fusion), channel_id=1, source_target_pairs={{0,2},{1,3},{2,0},{3,1},{4,6},{5,7},{6,4},{7,5},{8,10},{9,11},{10,... | collective-permute-start | bytes 393224 | tf_op jit(solution)/shard_map/ppermute | solution.py:40
  39.3 6.2 %collective-permute-start.3 = (f32[2,128,128]{2,1,0:T(8,128)S(1)}, f32[2,128,128]{2,1,0:T(8,128)S(1)}, u32[]{:S(2)}, u32[]{:S(2)}) collective-permute-start(f32[2,128,128]{2,1,0:T(8,128)S(1)} %pad_maximum_fusion.1), channel_id=1, source_target_pairs={{0,3},{1,2},{2,1},{3,0},{4,7},{5,6},{6,5},{7,4},{8,11},{9,10},{10,... | collective-permute-start | bytes 393224 | tf_op jit(solution)/shard_map/ppermute | solution.py:40
  40.3 5.4 %collective-permute-start.4 = (f32[2,128,128]{2,1,0:T(8,128)S(1)}, f32[2,128,128]{2,1,0:T(8,128)S(1)}, u32[]{:S(2)}, u32[]{:S(2)}) collective-permute-start(f32[2,128,128]{2,1,0:T(8,128)S(1)} %pad_maximum_fusion.2), channel_id=1, source_target_pairs={{0,1},{1,0},{2,3},{3,2},{4,5},{5,4},{6,7},{7,6},{8,9},{9,8},{10,11... | collective-permute-start | bytes 393224 | tf_op jit(solution)/shard_map/ppermute | solution.py:40
